TPU v7x, 512 devices: a whole 4x4x16 slice. The times are simulated.
512 devices in a mesh: dp: 128 (over y, z, x_lo), tensor: 4 (over x_hi, core).
Axes of the slice: x: 4 (x_hi: 2, x_lo: 2; x = x_hi * 2 + x_lo), y: 4, z: 16, core: 2. Of those that a mesh axis runs over, the one named last changes fastest.
Arguments:
- img_feat: bfloat16 [16384, 1280], P('dp'), may hold values from -8 to 8
- txt_feat: bfloat16 [16384, 1024], P('dp'), may hold values from -8 to 8
- img_proj: bfloat16 [1280, 512], P(None, 'tensor'), may hold values from -0.5 to 0.5
- txt_proj: bfloat16 [1024, 512], P(None, 'tensor'), may hold values from -0.5 to 0.5
- logit_scale: float32 [1], replicated, may hold values from 10 to 40
Outputs:
- grad_img_proj: float32 [1280, 512], P('dp', 'tensor')
- grad_txt_proj: float32 [1024, 512], P('dp', 'tensor')
- grad_img_feat: float32 [16384, 1280], P('dp', 'tensor')
- grad_txt_feat: float32 [16384, 1024], P('dp', 'tensor')
All inputs are finite; a program needn't handle non-finite values.
Results may differ from a plain program's by a relative error of at most 0.013.
Values may be sent and summed in bfloat16 or wider, within the bound.
A program may use at most 64 MiB of HBM per device.

v0:
```python
import jax
import jax.numpy as jnp
from jax import lax
from jax.sharding import PartitionSpec as P

eps = 1e-06
loss_factor = 256.0


def contract_last(left, right):
    return lax.dot_general(
        left, right, (((1,), (1,)), ((), ())), preferred_element_type=jnp.float32
    )


def differences(expo, totals, targets, key_ids):
    prob = expo / totals[:, None]
    onehot = (key_ids[None, :] == targets[:, None]).astype(jnp.float32)
    return (prob - onehot).astype(jnp.bfloat16)


def shards(img_feat, txt_feat, img_proj, txt_proj, logit_scale):
    rows = img_feat.shape[0]
    scale = logit_scale[0]
    n_data = lax.axis_size("dp")
    n_tensor = lax.axis_size("tensor")
    batch = rows * n_data
    coef = scale * loss_factor / (2.0 * batch)
    mine = lax.axis_index("dp")
    part_index = lax.axis_index("tensor")
    raw_img = jnp.dot(img_feat, img_proj, preferred_element_type=jnp.float32)
    raw_txt = jnp.dot(txt_feat, txt_proj, preferred_element_type=jnp.float32)
    square_img, square_txt = lax.psum(
        (jnp.sum(raw_img * raw_img, axis=1), jnp.sum(raw_txt * raw_txt, axis=1)), "tensor"
    )
    inv_img = lax.rsqrt(square_img + eps)[:, None]
    inv_txt = lax.rsqrt(square_txt + eps)[:, None]
    emb_img = (raw_img * inv_img).astype(jnp.bfloat16)
    emb_txt = (raw_txt * inv_txt).astype(jnp.bfloat16)
    targets = mine * rows + jnp.arange(rows, dtype=jnp.int32)
    full_img, full_txt = (
        lax.all_gather(emb_img, "tensor", axis=1, tiled=True),
        lax.all_gather(emb_txt, "tensor", axis=1, tiled=True),
    )
    cols_img, cols_txt = (
        lax.all_gather(emb_img, "dp", axis=0, tiled=True),
        lax.all_gather(emb_txt, "dp", axis=0, tiled=True),
    )
    keys_img, keys_txt = (
        lax.all_to_all(cols_img, "tensor", split_axis=0, concat_axis=1, tiled=True),
        lax.all_to_all(cols_txt, "tensor", split_axis=0, concat_axis=1, tiled=True),
    )
    share = batch // n_tensor
    key_ids = part_index * share + jnp.arange(share, dtype=jnp.int32)
    cos_img = contract_last(full_img, keys_txt)
    cos_txt = contract_last(full_txt, keys_img)
    expo_img = jnp.exp(scale * (cos_img - 1.0))
    expo_txt = jnp.exp(scale * (cos_txt - 1.0))
    total_img, total_txt = lax.psum(
        (jnp.sum(expo_img, axis=1), jnp.sum(expo_txt, axis=1)), "tensor"
    )
    diff_img = differences(expo_img, total_img, targets, key_ids)
    diff_txt = differences(expo_txt, total_txt, targets, key_ids)
    part_img = coef * jnp.dot(diff_img, keys_txt, preferred_element_type=jnp.float32)
    part_txt = coef * jnp.dot(diff_txt, keys_img, preferred_element_type=jnp.float32)
    grad_img, grad_txt = (
        lax.psum_scatter(part_img, "tensor", scatter_dimension=1, tiled=True),
        lax.psum_scatter(part_txt, "tensor", scatter_dimension=1, tiled=True),
    )
    align_img, align_txt = lax.psum(
        (
            jnp.sum(emb_img.astype(jnp.float32) * grad_img, axis=1),
            jnp.sum(emb_txt.astype(jnp.float32) * grad_txt, axis=1),
        ),
        "tensor",
    )
    grad_raw_img = ((grad_img - emb_img.astype(jnp.float32) * align_img[:, None]) * inv_img).astype(
        jnp.bfloat16
    )
    grad_raw_txt = ((grad_txt - emb_txt.astype(jnp.float32) * align_txt[:, None]) * inv_txt).astype(
        jnp.bfloat16
    )
    term_img = lax.dot_general(
        img_feat, grad_raw_img, (((0,), (0,)), ((), ())), preferred_element_type=jnp.float32
    )
    term_txt = lax.dot_general(
        txt_feat, grad_raw_txt, (((0,), (0,)), ((), ())), preferred_element_type=jnp.float32
    )
    grad_img_proj, grad_txt_proj = (
        lax.psum_scatter(term_img, "dp", scatter_dimension=0, tiled=True),
        lax.psum_scatter(term_txt, "dp", scatter_dimension=0, tiled=True),
    )
    back_img = contract_last(grad_raw_img, img_proj)
    back_txt = contract_last(grad_raw_txt, txt_proj)
    grad_img_feat, grad_txt_feat = (
        lax.psum_scatter(
            back_img.astype(jnp.bfloat16), "tensor", scatter_dimension=1, tiled=True
        ).astype(jnp.float32),
        lax.psum_scatter(
            back_txt.astype(jnp.bfloat16), "tensor", scatter_dimension=1, tiled=True
        ).astype(jnp.float32),
    )
    return (grad_img_proj, grad_txt_proj, grad_img_feat, grad_txt_feat)


def solution(mesh):
    return jax.shard_map(
        shards,
        mesh=mesh,
        in_specs=(P("dp", None), P("dp", None), P(None, "tensor"), P(None, "tensor"), P()),
        out_specs=(P("dp", "tensor"), P("dp", "tensor"), P("dp", "tensor"), P("dp", "tensor")),
        check_vma=False,
    )
```

profile of v0, /device:TPU:2, one launch (start us, length us, event | category | flops | bytes accessed | tf_op | source)
XLA Modules:
  0.0 2343.4 jit_solution(8423834895408553254)
XLA Ops:
  8.1 1.3 multiply_reduce_fusion.1
  9.4 1.3 multiply_reduce_fusion
  10.8 9.0 all-reduce.5
  21.2 466.2 %all-gather.3.cloned.1.call-done = bf16[16384,128]{0,1:T(8,128)(2,1)} async-done(((bf16[128,128]{0,1:T(8,128)(2,1)}), bf16[16384,128]{0,1:T(8,128)(2,1)}) %all-gather.3.cloned.1.call-update) | async-done | bytes 4194320 | tf_op jit(solution)/shard_map/all_gather | solution.py:47
  487.4 4.7 copy.36
  492.1 4.9 all-to-all-start
  496.9 455.3 %all-gather.5.cloned.1.call-done = bf16[16384,128]{0,1:T(8,128)(2,1)} async-done(((bf16[128,128]{0,1:T(8,128)(2,1)}), bf16[16384,128]{0,1:T(8,128)(2,1)}) %all-gather.5.cloned.1.call-update) | async-done | bytes 4194320 | tf_op jit(solution)/shard_map/all_gather | solution.py:46
  952.3 4.6 copy.35
  956.9 5.0 all-to-all-start.1
  962.6 50.4 %all_gather.14 = bf16[128,512]{0,1:T(8,128)(2,1)S(1)} all-gather(bf16[128,128]{0,1:T(8,128)(2,1)S(1)} %copy-done.4), channel_id=1, replica_groups=mesh['dp'=128,'tensor'=4] {'tensor'}, dimensions={1}, use_global_device_ids=true | all-gather | bytes 163840 | tf_op jit(solution)/shard_map/all_gather | solution.py:43
  1013.1 6.9 all_gather.12
  1020.0 3.2 fusion.20
  1023.2 4.5 fusion.21
  1027.8 7.5 all-reduce.4
  1035.2 4.9 convolution_multiply_fusion
  1040.2 4.3 convolution_multiply_fusion.1
  1044.6 32.2 %reduce-scatter.9.cloned.1.call-done = f32[128,128]{0,1:T(8,128)} async-done(((f32[128,512]{0,1:T(8,128)}), f32[128,128]{0,1:T(8,128)}) %reduce-scatter.9.cloned.1.call-update) | async-done | bytes 65552 | tf_op jit(solution)/shard_map/reduce_scatter | solution.py:68
  1077.7 44.2 %reduce-scatter.7.cloned.1.call-done = f32[128,128]{0,1:T(8,128)} async-done(((f32[128,512]{0,1:T(8,128)}), f32[128,128]{0,1:T(8,128)}) %reduce-scatter.7.cloned.1.call-update) | async-done | bytes 65552 | tf_op jit(solution)/shard_map/reduce_scatter | solution.py:67
  1122.7 8.0 all-reduce.3
  1138.4 37.2 %reduce-scatter.13.cloned.1.call-done = bf16[128,256]{1,0:T(8,128)(2,1)} async-done(((bf16[128,1024]{1,0:T(8,128)(2,1)}), bf16[128,256]{1,0:T(8,128)(2,1)}) %reduce-scatter.13.cloned.1.call-update) | async-done | bytes 65552 | tf_op jit(solution)/shard_map/reduce_scatter | solution.py:99
  1175.6 1.5 convert_element_type.54
  1177.1 44.0 %reduce-scatter.11.cloned.1.call-done = bf16[128,320]{0,1:T(8,128)(2,1)} async-done(((bf16[128,1280]{0,1:T(8,128)(2,1)}), bf16[128,320]{0,1:T(8,128)(2,1)}) %reduce-scatter.11.cloned.1.call-update) | async-done | bytes 81936 | tf_op jit(solution)/shard_map/reduce_scatter | solution.py:96
  1221.1 1.6 convert_element_type.52
  1222.6 1110.7 %all-reduce.8.cloned.1.call-done = (f32[1280,128]{0,1:T(8,128)}, f32[1024,128]{0,1:T(8,128)}) async-done(((f32[1280,128]{0,1:T(8,128)}, f32[1024,128]{0,1:T(8,128)}), (f32[1280,128]{0,1:T(8,128)}, f32[1024,128]{0,1:T(8,128)})) %all-reduce.8.cloned.1.call-update) | async-done | bytes 1179664
  (46 shorter events, 13.9 us)
Async XLA Ops:
  7.2 1.0 copy-start
  7.2 480.2 %all-gather.3.cloned.1.call-start = ((), (), s32[]{:S(2)}) async-start(), calls=%async_computation.6 | async-start | bytes 4227072 | tf_op jit(solution)/shard_map/all_gather | solution.py:47
  20.5 931.8 %all-gather.5.cloned.1.call-start = ((), (), s32[]{:S(2)}) async-start(), calls=%async_computation.8 | async-start | bytes 4227072 | tf_op jit(solution)/shard_map/all_gather | solution.py:46
  492.1 464.9 %all-to-all-start = ((bf16[4,4096,128]{1,2,0:T(8,128)(2,1)}), bf16[4,4096,128]{1,2,0:T(8,128)(2,1)}, u32[]{:S(2)}, u32[]{:S(2)}) async-start(bf16[4,4096,128]{1,2,0:T(8,128)(2,1)} %bitcast.46), calls=%async_computation | async-start | bytes 8388608 | tf_op jit(solution)/shard_map/all_to_all | solution.py:51
  956.9 5.7 copy-start.4
  956.9 56.2 %copy-start.5 = (bf16[128,128]{0,1:T(8,128)(2,1)S(1)}, bf16[128,128]{0,1:T(8,128)(2,1)}, u32[]{:S(2)}) copy-start(bf16[128,128]{0,1:T(8,128)(2,1)} %multiply_convert_fusion.1) | copy-start | bytes 98308
  956.9 66.3 %all-to-all-start.1 = ((bf16[4,4096,128]{1,2,0:T(8,128)(2,1)}), bf16[4,4096,128]{1,2,0:T(8,128)(2,1)}, u32[]{:S(2)}, u32[]{:S(2)}) async-start(bf16[4,4096,128]{1,2,0:T(8,128)(2,1)} %bitcast.45), calls=%async_computation.2 | async-start | bytes 8388608 | tf_op jit(solution)/shard_map/all_to_all | solution.py:50
  961.9 114.9 %reduce-scatter.9.cloned.1.call-start = ((), (), s32[]{:S(2)}) async-start(), calls=%async_computation.9 | async-start | bytes 327680 | tf_op jit(solution)/shard_map/reduce_scatter | solution.py:68
  1040.2 81.7 %reduce-scatter.7.cloned.1.call-start = ((), (), s32[]{:S(2)}) async-start(), calls=%async_computation.7 | async-start | bytes 327680 | tf_op jit(solution)/shard_map/reduce_scatter | solution.py:67
  1040.2 91.4 %copy-start.3 = (bf16[1024,128]{1,0:T(8,128)(2,1)S(1)}, bf16[1024,128]{1,0:T(8,128)(2,1)}, u32[]{:S(2)}) copy-start(bf16[1024,128]{1,0:T(8,128)(2,1)} %param.8) | copy-start | bytes 786436
  1044.5 89.2 %copy-start.2 = (bf16[128,1024]{1,0:T(8,128)(2,1)S(1)}, bf16[128,1024]{1,0:T(8,128)(2,1)}, u32[]{:S(2)}) copy-start(bf16[128,1024]{1,0:T(8,128)(2,1)} %param.6) | copy-start | bytes 786436
  1044.5 90.2 %copy-start.1 = (bf16[128,1280]{1,0:T(8,128)(2,1)S(1)}, bf16[128,1280]{1,0:T(8,128)(2,1)}, u32[]{:S(2)}) copy-start(bf16[128,1280]{1,0:T(8,128)(2,1)} %param.5) | copy-start | bytes 983044
  1044.5 131.1 %reduce-scatter.13.cloned.1.call-start = ((), (), s32[]{:S(2)}) async-start(), calls=%async_computation.11 | async-start | bytes 327680 | tf_op jit(solution)/shard_map/reduce_scatter | solution.py:99
  1132.6 88.5 %reduce-scatter.11.cloned.1.call-start = ((), (), s32[]{:S(2)}) async-start(), calls=%async_computation.10 | async-start | bytes 409600 | tf_op jit(solution)/shard_map/reduce_scatter | solution.py:96
  1133.6 1199.7 %all-reduce.8.cloned.1.call-start = ((), (), s32[]{:S(2)}) async-start(), calls=%async_computation.12 | async-start | bytes 2359296
Sparse Core Ops, SparseCore 0:
  20.6 466.7 all-gather.2
  490.0 462.2 all-gather.4
  1040.3 36.4 reduce-scatter.8
  1079.9 41.8 reduce-scatter.6
  1132.7 42.8 reduce-scatter.12
  1178.7 42.2 reduce-scatter.10
  1224.1 1109.2 all-reduce.7
where the time goes:
time: 2340 us
  waiting for transfers between devices  2190 us (94%)
  blocking collectives  81.9 us (4%)
  matrix products  23.5 us (1%)
    unnamed x8, waiting for transfers between devices  1110 us
    all_gather x1, waiting for transfers between devices, shards(): lax.all_gather(emb_txt, 'dp', axis=0, tiled=True)  466 us
    all_gather x1, waiting for transfers between devices, shards(): lax.all_gather(emb_img, 'dp', axis=0, tiled=True)  455 us
    all_gather x1, blocking collectives, shards(): lax.all_gather(emb_txt, 'tensor', axis=1, tiled=True)  50.4 us
  transfers between devices with their start and end apart: 9, of which 7 were waited for; matrix products, arithmetic and copies ran while one was open for 1% of the time, Pallas kernels for 0%

commit v1 on v0

v1 whole, which is shorter than its diff:
```python
import functools

import jax
import jax.numpy as jnp
from jax import lax
from jax.experimental import pallas as pl
from jax.experimental.pallas import tpu as pltpu
from jax.sharding import PartitionSpec as P

Z = 16
XL = 2
T = 4
ROWS = 128
Q = 128
SUMS = 16
PIECE = ROWS + SUMS
eps = 1e-06
loss_factor = 256.0
f32 = jnp.float32
bf16 = jnp.bfloat16


def nt(left, right):
    return lax.dot_general(left, right, (((1,), (1,)), ((), ())), preferred_element_type=f32)


def tn(left, right):
    return lax.dot_general(left, right, (((0,), (0,)), ((), ())), preferred_element_type=f32)


def row_sums(values):
    return jnp.sum(jnp.transpose(values), axis=0, keepdims=True)


def as_columns(row):
    return jnp.transpose(jnp.broadcast_to(row, (ROWS, ROWS)))


def pack_sums(off, diag):
    index = lax.broadcasted_iota(jnp.int32, (SUMS, ROWS), 0)
    off_hi = off.astype(bf16).astype(f32)
    diag_hi = diag.astype(bf16).astype(f32)
    parts = jnp.where(
        index == 0,
        off_hi,
        jnp.where(
            index == 1,
            off - off_hi,
            jnp.where(index == 2, diag_hi, jnp.where(index == 3, diag - diag_hi, 0.0)),
        ),
    )
    return parts.astype(bf16)


def unpack_sums(parts):
    return parts[0:1] + parts[1:2], parts[2:3] + parts[3:4]


def window_of(per):
    return max(-(-(((k * per) % 8) + per) // 8) * 8 for k in range(8))


def kernel(
    ny, di, dt,
    scale_ref, imgf, txtf, imgp, txtp,
    gip, gtp, gif, gtf,
    sqb, invc, own, img_all, zbuf, txt_all,
    psi, pst, gt_acc, col_acc,
    rs_send, rs_recv, gx_send, gz, f_send, f_recv, b_send, b_recv,
    alb, gr_own, gr_all, y_send, y_recv, x_send, x_recv, zsum, z_send, z_recv,
    sq_ss, sq_rs, pp_ss, pp_rs, ig_ss, ig_rs, zf_ss, zf_rs, zb_ss, zb_rs,
    tx_ss, tx_rs, ri_ss, ri_rs, gx_ss, gx_rs, f_ss, f_rs, b_ss, b_rs,
    al_ss, al_rs, gr_ss, gr_rs, y_ss, y_rs, x_ss, x_rs, z_ss, z_rs,
):
    n_blocks = ny * XL
    n_plane = n_blocks * T
    half = Z // 2
    batch = ny * Z * XL * ROWS
    dp = lax.axis_index("dp")
    t = lax.axis_index("tensor")
    xl = dp % XL
    z = (dp // XL) % Z
    y = dp // (XL * Z)
    b = y * XL + xl
    p = b * T + t

    def plane_dev(q):
        block = q // T
        return (((block // XL) * Z + z) * XL + block % XL, q % T)

    def z_dev(other):
        return ((y * Z + other) * XL + xl, t)

    def y_dev(other):
        return ((other * Z + z) * XL + xl, t)

    def t_dev(other):
        return (dp, other)

    def remote(src, dst, send, recv, dev):
        return pltpu.make_async_remote_copy(
            src_ref=src, dst_ref=dst, send_sem=send, recv_sem=recv,
            device_id=dev, device_id_type=pl.DeviceIdType.MESH,
        )

    barrier = pltpu.get_barrier_semaphore()

    @pl.loop(1, n_plane)
    def _(i):
        pl.semaphore_signal(
            barrier, inc=1, device_id=plane_dev((p + i) % n_plane),
            device_id_type=pl.DeviceIdType.MESH,
        )

    @pl.loop(1, Z)
    def _(i):
        pl.semaphore_signal(
            barrier, inc=1, device_id=z_dev((z + i) % Z), device_id_type=pl.DeviceIdType.MESH
        )

    scale = scale_ref[0]
    coef = scale * (loss_factor / (2.0 * batch))

    raw_img = jnp.dot(imgf[...], imgp[...], preferred_element_type=f32)
    raw_txt = jnp.dot(txtf[...], txtp[...], preferred_element_type=f32)
    index8 = lax.broadcasted_iota(jnp.int32, (8, ROWS), 0)
    sqb[t] = jnp.where(
        index8 == 0, row_sums(raw_img * raw_img), row_sums(raw_txt * raw_txt)
    )
    pl.semaphore_wait(barrier, n_plane - 1 + Z - 1)

    def sq_copy(i):
        return remote(sqb.at[t], sqb.at[t], sq_ss.at[i - 1], sq_rs.at[t], t_dev((t + i) % T))

    def sq_wait(i):
        src = (t + i) % T
        return remote(sqb.at[src], sqb.at[src], sq_ss.at[i - 1], sq_rs.at[src], t_dev(src))

    for i in range(1, T):
        sq_copy(i).start()
    for i in range(1, T):
        sq_wait(i).wait_recv()
    square = (sqb[0] + sqb[1]) + (sqb[2] + sqb[3])
    inv = lax.rsqrt(square + eps)
    inv_img = as_columns(inv[0:1])
    inv_txt = as_columns(inv[1:2])
    invc[0] = inv_img
    invc[1] = inv_txt
    emb_img = (raw_img * inv_img).astype(bf16)
    emb_txt = (raw_txt * inv_txt).astype(bf16)
    own[0] = emb_img
    own[1] = emb_txt
    zbuf[z] = emb_txt

    def img_slot(q):
        return img_all.at[
            pl.ds(pl.multiple_of((q // T) * ROWS, ROWS), ROWS),
            pl.ds(pl.multiple_of((q % T) * Q, Q), Q),
        ]

    def txt_slot(k, quarter):
        return txt_all.at[
            pl.ds(pl.multiple_of(k * ROWS, ROWS), ROWS),
            pl.ds(pl.multiple_of(quarter * Q, Q), Q),
        ]

    def zf_copy(s):
        piece = (z - s + Z) % Z
        return remote(zbuf.at[piece], zbuf.at[piece], zf_ss.at[s], zf_rs.at[s], z_dev((z + 1) % Z))

    def zf_land(s):
        piece = (z - 1 - s + 2 * Z) % Z
        return remote(zbuf.at[piece], zbuf.at[piece], zf_ss.at[s], zf_rs.at[s], z_dev((z + 1) % Z))

    def zb_copy(s):
        piece = (z + s) % Z
        return remote(zbuf.at[piece], zbuf.at[piece], zb_ss.at[s], zb_rs.at[s], z_dev((z - 1 + Z) % Z))

    def zb_land(s):
        piece = (z + 1 + s) % Z
        return remote(zbuf.at[piece], zbuf.at[piece], zb_ss.at[s], zb_rs.at[s], z_dev((z - 1 + Z) % Z))

    def tx_remote(piece):
        return remote(
            zbuf.at[piece], txt_slot(piece // T, t), tx_ss.at[piece],
            tx_rs.at[(piece // T) * T + t], t_dev(piece % T),
        )

    def tx_local(piece):
        return pltpu.make_async_copy(zbuf.at[piece], txt_slot(piece // T, t), tx_ss.at[piece])

    def pass_on(piece):
        @pl.when(piece % T != t)
        def _():
            tx_remote(piece).start()

        @pl.when(piece % T == t)
        def _():
            tx_local(piece).start()

    zf_copy(0).start()
    zb_copy(0).start()
    pass_on(z)

    own_img_copy = pltpu.make_async_copy(own.at[0], img_slot(p), ig_ss.at[0])
    own_img_copy.start()

    def ig_copy(i):
        return remote(own.at[0], img_slot(p), ig_ss.at[i], ig_rs.at[p], plane_dev((p + i) % n_plane))

    @pl.loop(1, n_plane)
    def _(i):
        ig_copy(i).start()

    di4, dt4 = di // T, dt // T

    def pp_copies(i):
        dst = (t + i) % T
        return (
            remote(
                imgp.at[pl.ds(pl.multiple_of(dst * di4, di4), di4), :],
                psi.at[:, pl.ds(pl.multiple_of(t * Q, Q), Q)],
                pp_ss.at[2 * i], pp_rs.at[2 * t], t_dev(dst),
            ),
            remote(
                txtp.at[pl.ds(pl.multiple_of(dst * dt4, dt4), dt4), :],
                pst.at[:, pl.ds(pl.multiple_of(t * Q, Q), Q)],
                pp_ss.at[2 * i + 1], pp_rs.at[2 * t + 1], t_dev(dst),
            ),
        )

    def pp_lands(i):
        src = (t + i) % T
        return (
            remote(
                imgp.at[pl.ds(0, di4), :], psi.at[:, pl.ds(pl.multiple_of(src * Q, Q), Q)],
                pp_ss.at[2 * i], pp_rs.at[2 * src], t_dev(src),
            ),
            remote(
                txtp.at[pl.ds(0, dt4), :], pst.at[:, pl.ds(pl.multiple_of(src * Q, Q), Q)],
                pp_ss.at[2 * i + 1], pp_rs.at[2 * src + 1], t_dev(src),
            ),
        )

    own_psi = pltpu.make_async_copy(
        imgp.at[pl.ds(pl.multiple_of(t * di4, di4), di4), :],
        psi.at[:, pl.ds(pl.multiple_of(t * Q, Q), Q)], pp_ss.at[0],
    )
    own_pst = pltpu.make_async_copy(
        txtp.at[pl.ds(pl.multiple_of(t * dt4, dt4), dt4), :],
        pst.at[:, pl.ds(pl.multiple_of(t * Q, Q), Q)], pp_ss.at[1],
    )
    own_psi.start()
    own_pst.start()

    @pl.loop(1, half)
    def _(s):
        zf_land(s - 1).wait_recv()
        zf_copy(s).start()
        pass_on((z - s + Z) % Z)
        zb_land(s - 1).wait_recv()

        @pl.when(s < half - 1)
        def _():
            zb_copy(s).start()

        pass_on((z + s) % Z)

    zf_land(half - 1).wait_recv()
    pass_on((z - half + Z) % Z)

    @pl.loop(1, T)
    def _(i):
        for copy in pp_copies(i):
            copy.start()

    own_img_copy.wait()

    @pl.loop(1, n_plane)
    def _(i):
        src = (p + i) % n_plane
        remote(own.at[0], img_slot(src), ig_ss.at[i], ig_rs.at[src], plane_dev(src)).wait_recv()

    @pl.loop(0, Z)
    def _(piece):
        @pl.when(piece % T == t)
        def _():
            tx_local(piece).wait()

    @pl.loop(0, Z // T)
    def _(k):
        for i in range(1, T):
            src = (t + i) % T
            remote(
                zbuf.at[0], txt_slot(k, src), tx_ss.at[0], tx_rs.at[k * T + src], t_dev(src)
            ).wait_recv()

    keys = Z // T * ROWS
    gt_acc[...] = jnp.zeros_like(gt_acc)
    col_acc[...] = jnp.zeros_like(col_acc)

    def rs_copy(block, quarter):
        q = block * T + quarter
        return remote(rs_send.at[q], rs_recv.at[p], ri_ss.at[q], ri_rs.at[p], plane_dev(q))

    def masked_diag(cond):
        i = lax.broadcasted_iota(jnp.int32, (ROWS, keys), 0)
        j = lax.broadcasted_iota(jnp.int32, (ROWS, keys), 1)
        shift = jnp.where(cond, (z // T) * ROWS, -2 * ROWS)
        return (j - i) == shift

    @pl.loop(0, n_blocks)
    def _(n):
        block = (b + 1 + n) % n_blocks
        rows = img_all[pl.ds(pl.multiple_of(block * ROWS, ROWS), ROWS), :]
        cos = nt(rows, txt_all[...])
        expo = jnp.exp(scale * (cos - 1.0))
        mask = masked_diag((block == b) & (t == z % T))
        off = jnp.where(mask, 0.0, expo)
        on = jnp.where(mask, expo, 0.0)
        diag = jnp.sum(on, axis=0, keepdims=True)
        diag = sum(diag[:, k * ROWS:(k + 1) * ROWS] for k in range(keys // ROWS))
        folded = sum(off[:, k * ROWS:(k + 1) * ROWS] for k in range(keys // ROWS))
        sums = pack_sums(row_sums(folded), diag)
        col_acc[0:1, :] += jnp.sum(off, axis=0, keepdims=True)
        col_acc[1:2, :] += jnp.sum(on, axis=0, keepdims=True)
        weights = off.astype(bf16)
        part = jnp.dot(weights, txt_all[...], preferred_element_type=f32)
        for quarter in range(T):
            q = block * T + quarter
            rs_send[q, 0:ROWS, :] = part[:, quarter * Q:(quarter + 1) * Q].astype(bf16)
            rs_send[q, ROWS:PIECE, :] = sums

        for quarter in range(T):
            @pl.when(block * T + quarter != p)
            def _(quarter=quarter):
                rs_copy(block, quarter).start()

        gt_acc[...] += tn(weights, rows)

    def gx_copy(k, i):
        dst = (t + i) % T
        return remote(
            gx_send.at[k * T + dst], gz.at[k * T + t], gx_ss.at[k * T + dst],
            gx_rs.at[k * T + t], t_dev(dst),
        )

    for k in range(Z // T):
        sums = pack_sums(
            col_acc[0:1, k * ROWS:(k + 1) * ROWS], col_acc[1:2, k * ROWS:(k + 1) * ROWS]
        )
        for quarter in range(T):
            gx_send[k * T + quarter, 0:ROWS, :] = gt_acc[
                k * ROWS:(k + 1) * ROWS, quarter * Q:(quarter + 1) * Q
            ].astype(bf16)
            gx_send[k * T + quarter, ROWS:PIECE, :] = sums
        for i in range(1, T):
            gx_copy(k, i).start()
        gz[k * T + t] = gx_send[k * T + t]

    @pl.loop(0, Z // T)
    def _(k):
        for i in range(1, T):
            src = (t + i) % T
            remote(
                gx_send.at[0], gz.at[k * T + src], gx_ss.at[0], gx_rs.at[k * T + src], t_dev(src)
            ).wait_recv()

    def f_copy(s):
        return remote(f_send.at[s], f_recv.at[s], f_ss.at[s], f_rs.at[s], z_dev((z + 1) % Z))

    def b_copy(s):
        return remote(b_send.at[s], b_recv.at[s], b_ss.at[s], b_rs.at[s], z_dev((z - 1 + Z) % Z))

    def added(left, right):
        total = left[0:ROWS].astype(f32) + right[0:ROWS].astype(f32)
        off, diag = unpack_sums(left[ROWS:PIECE].astype(f32) + right[ROWS:PIECE].astype(f32))
        return total.astype(bf16), pack_sums(off, diag)

    f_send[0] = gz[(z + half) % Z]
    f_copy(0).start()
    b_send[0] = gz[(z + half + 1) % Z]
    b_copy(0).start()

    @pl.loop(1, half)
    def _(s):
        f_copy(s - 1).wait_recv()
        main, sums = added(f_recv[s - 1], gz[(z + half - s) % Z])
        f_send[s, 0:ROWS, :] = main
        f_send[s, ROWS:PIECE, :] = sums
        f_copy(s).start()

        @pl.when(s < half - 1)
        def _():
            b_copy(s - 1).wait_recv()
            main, sums = added(b_recv[s - 1], gz[(z + half + 1 + s) % Z])
            b_send[s, 0:ROWS, :] = main
            b_send[s, ROWS:PIECE, :] = sums
            b_copy(s).start()

    def rs_sum(i, carry):
        total, sums = carry
        src = (p + i) % n_plane
        remote(rs_send.at[0], rs_recv.at[src], ri_ss.at[0], ri_rs.at[src], plane_dev(src)).wait_recv()
        return (
            total + rs_recv[src, 0:ROWS, :].astype(f32),
            sums + rs_recv[src, ROWS:PIECE, :].astype(f32),
        )

    total_img, sums_img = lax.fori_loop(
        1, n_plane, rs_sum,
        (rs_send[p, 0:ROWS, :].astype(f32), rs_send[p, ROWS:PIECE, :].astype(f32)),
    )
    f_copy(half - 1).wait_recv()
    b_copy(half - 2).wait_recv()
    total_txt = (
        gz[z, 0:ROWS, :].astype(f32)
        + f_recv[half - 1, 0:ROWS, :].astype(f32)
        + b_recv[half - 2, 0:ROWS, :].astype(f32)
    )
    sums_txt = (
        gz[z, ROWS:PIECE, :].astype(f32)
        + f_recv[half - 1, ROWS:PIECE, :].astype(f32)
        + b_recv[half - 2, ROWS:PIECE, :].astype(f32)
    )

    def embedding_grad(total, sums, target):
        off, diag = unpack_sums(sums)
        factor = as_columns(coef / (off + diag))
        return factor * (total - as_columns(off) * target)

    own_img = own[0].astype(f32)
    own_txt = own[1].astype(f32)
    g_img = embedding_grad(total_img, sums_img, own_txt)
    g_txt = embedding_grad(total_txt, sums_txt, own_img)

    def al_copy(i):
        return remote(alb.at[t], alb.at[t], al_ss.at[i - 1], al_rs.at[t], t_dev((t + i) % T))

    alb[t] = jnp.where(index8 == 0, row_sums(own_img * g_img), row_sums(own_txt * g_txt))
    for i in range(1, T):
        al_copy(i).start()
    for i in range(1, T):
        src = (t + i) % T
        remote(alb.at[src], alb.at[src], al_ss.at[i - 1], al_rs.at[src], t_dev(src)).wait_recv()
    align = (alb[0] + alb[1]) + (alb[2] + alb[3])
    gr_img = ((g_img - own_img * as_columns(align[0:1])) * invc[0]).astype(bf16)
    gr_txt = ((g_txt - own_txt * as_columns(align[1:2])) * invc[1]).astype(bf16)
    gr_own[0] = gr_img
    gr_own[1] = gr_txt

    def gr_copy(m, i):
        return remote(
            gr_own.at[m], gr_all.at[m, :, pl.ds(pl.multiple_of(t * Q, Q), Q)],
            gr_ss.at[m * T + i], gr_rs.at[m * T + t], t_dev((t + i) % T),
        )

    own_gr = []
    for m in range(2):
        for i in range(1, T):
            gr_copy(m, i).start()
        own_gr.append(
            pltpu.make_async_copy(
                gr_own.at[m], gr_all.at[m, :, pl.ds(pl.multiple_of(t * Q, Q), Q)], gr_ss.at[m * T]
            )
        )
        own_gr[m].start()

    diy, dty = di // ny, dt // ny
    for k in range(ny):
        for c in range(0, diy, 64):
            y_send[k, c:c + 64, :] = tn(
                imgf[:, k * diy + c:k * diy + c + 64], gr_img
            ).astype(bf16)
        for c in range(0, dty, 64):
            y_send[k, diy + c:diy + c + 64, :] = tn(
                txtf[:, k * dty + c:k * dty + c + 64], gr_txt
            ).astype(bf16)

    def y_copy(i):
        dst = (y + i) % ny
        return remote(y_send.at[dst], y_recv.at[y], y_ss.at[i], y_rs.at[y], y_dev(dst))

    for i in range(1, ny):
        y_copy(i).start()

    for m in range(2):
        own_gr[m].wait()
        for i in range(1, T):
            src = (t + i) % T
            remote(
                gr_own.at[m], gr_all.at[m, :, pl.ds(pl.multiple_of(src * Q, Q), Q)],
                gr_ss.at[m * T + i], gr_rs.at[m * T + src], t_dev(src),
            ).wait_recv()
    own_psi.wait()
    own_pst.wait()

    @pl.loop(1, T)
    def _(i):
        for copy in pp_lands(i):
            copy.wait_recv()

    gif[...] = nt(gr_all[0], psi[...])
    gtf[...] = nt(gr_all[1], pst[...])

    zsum[...] = y_send[y].astype(f32)
    for i in range(1, ny):
        src = (y + i) % ny
        remote(y_send.at[0], y_recv.at[src], y_ss.at[i], y_rs.at[src], y_dev(src)).wait_recv()
        zsum[...] += y_recv[src].astype(f32)
    x_send[...] = zsum[...].astype(bf16)
    x_dev = (dp - xl + (XL - 1 - xl), t)
    x_copy = remote(x_send, x_recv, x_ss.at[0], x_rs.at[0], x_dev)
    if XL == 2:
        x_copy.start()
        x_copy.wait_recv()
        zsum[...] = x_send[...].astype(f32) + x_recv[...].astype(f32)

    per_i, per_t = diy // (Z * XL), dty // (Z * XL)
    win = window_of(per_i)

    def z_copy(i):
        dst = (z + i) % Z
        return remote(z_send.at[dst], z_recv.at[z], z_ss.at[i], z_rs.at[z], z_dev(dst))

    @pl.loop(0, Z)
    def _(i):
        dst = (z + i) % Z
        first = ((dst * XL + xl) * per_i) // 8 * 8
        z_send[dst, 0:win, :] = zsum[pl.ds(pl.multiple_of(first, 8), win), :]
        z_send[dst, win:win + per_t, :] = zsum[
            pl.ds(pl.multiple_of(diy + (dst * XL + xl) * per_t, 8), per_t), :
        ]

        @pl.when(i > 0)
        def _():
            z_copy(i).start()

    def z_add(i, total):
        src = (z + i) % Z
        remote(z_send.at[0], z_recv.at[src], z_ss.at[i], z_rs.at[src], z_dev(src)).wait_recv()
        return total + z_recv[src]

    total = lax.fori_loop(1, Z, z_add, z_send[z])
    shift = ((z * XL + xl) * per_i) % 8
    result = total[0:per_i]
    for k in sorted({(k * per_i) % 8 for k in range(8)} - {0}):
        result = jnp.where(shift == k, total[k:k + per_i], result)
    gip[...] = result
    gtp[...] = total[win:win + per_t]

    for i in range(1, T):
        sq_copy(i).wait_send()
        al_copy(i).wait_send()
        for copy in pp_copies(i):
            copy.wait_send()
        for m in range(2):
            gr_copy(m, i).wait_send()
        for k in range(Z // T):
            gx_copy(k, i).wait_send()

    @pl.loop(1, n_plane)
    def _(i):
        ig_copy(i).wait_send()
        q = (p + i) % n_plane
        rs_copy(q // T, q % T).wait_send()

    @pl.loop(0, half)
    def _(s):
        zf_copy(s).wait_send()
        f_copy(s).wait_send()

    @pl.loop(0, half - 1)
    def _(s):
        zb_copy(s).wait_send()
        b_copy(s).wait_send()

    @pl.loop(0, Z)
    def _(piece):
        @pl.when(piece % T != t)
        def _():
            tx_remote(piece).wait_send()

    for i in range(1, ny):
        y_copy(i).wait_send()
    if XL == 2:
        x_copy.wait_send()

    @pl.loop(1, Z)
    def _(i):
        z_copy(i).wait_send()


def shards(ny, img_feat, txt_feat, img_proj, txt_proj, logit_scale):
    di, dt = img_feat.shape[1], txt_feat.shape[1]
    n_blocks = ny * XL
    n_plane = n_blocks * T
    keys = Z // T * ROWS
    emb = T * Q
    half = Z // 2
    ndp = ny * Z * XL
    diy, dty = di // ny, dt // ny
    win = window_of(diy // (Z * XL))
    per_t = dty // (Z * XL)
    dma = pltpu.SemaphoreType.DMA
    vmem = pltpu.VMEM
    scratch = [
        vmem((T, 8, ROWS), f32),
        vmem((2, ROWS, Q), f32),
        vmem((2, ROWS, Q), bf16),
        vmem((n_blocks * ROWS, emb), bf16),
        vmem((Z, ROWS, Q), bf16),
        vmem((keys, emb), bf16),
        vmem((di // T, emb), bf16),
        vmem((dt // T, emb), bf16),
        vmem((keys, emb), f32),
        vmem((8, keys), f32),
        vmem((n_plane, PIECE, Q), bf16),
        vmem((n_plane, PIECE, Q), bf16),
        vmem((Z, PIECE, Q), bf16),
        vmem((Z, PIECE, Q), bf16),
        vmem((half, PIECE, Q), bf16),
        vmem((half, PIECE, Q), bf16),
        vmem((half, PIECE, Q), bf16),
        vmem((half, PIECE, Q), bf16),
        vmem((T, 8, ROWS), f32),
        vmem((2, ROWS, Q), bf16),
        vmem((2, ROWS, emb), bf16),
        vmem((ny, diy + dty, Q), bf16),
        vmem((ny, diy + dty, Q), bf16),
        vmem((diy + dty, Q), bf16),
        vmem((diy + dty, Q), bf16),
        vmem((diy + dty, Q), f32),
        vmem((Z, win + per_t, Q), f32),
        vmem((Z, win + per_t, Q), f32),
    ]
    sems = [
        T, T, 2 * T, 2 * T, n_plane, n_plane, half, half, half, half,
        Z, Z, n_plane, n_plane, Z, Z, half, half, half, half,
        T, T, 2 * T, 2 * T, max(ny, 2), max(ny, 2), 1, 1, Z, Z,
    ]
    scratch += [dma((n,)) for n in sems]
    whole = pl.BlockSpec(memory_space=pltpu.VMEM)
    return pl.pallas_call(
        functools.partial(kernel, ny, di, dt),
        out_shape=(
            jax.ShapeDtypeStruct((di // ndp, Q), f32),
            jax.ShapeDtypeStruct((dt // ndp, Q), f32),
            jax.ShapeDtypeStruct((ROWS, di // T), f32),
            jax.ShapeDtypeStruct((ROWS, dt // T), f32),
        ),
        in_specs=[pl.BlockSpec(memory_space=pltpu.SMEM)] + [whole] * 4,
        out_specs=(whole,) * 4,
        scratch_shapes=scratch,
        compiler_params=pltpu.CompilerParams(
            collective_id=0, has_side_effects=True, vmem_limit_bytes=48 * 1024 * 1024
        ),
    )(logit_scale, img_feat, txt_feat, img_proj, txt_proj)


def solution(mesh):
    ny = mesh.shape["dp"] // (Z * XL)
    return jax.shard_map(
        functools.partial(shards, ny),
        mesh=mesh,
        in_specs=(P("dp", None), P("dp", None), P(None, "tensor"), P(None, "tensor"), P()),
        out_specs=(P("dp", "tensor"), P("dp", "tensor"), P("dp", "tensor"), P("dp", "tensor")),
        check_vma=False,
    )
```

time: 2340 us -> 140 us (0.06)
  the two profiles are of different devices: /device:TPU:2 before, /device:TPU:1 now
where the time goes in v1:
time: 140 us; the launch traced here: 139 us
  Pallas kernels  131 us (94%)
  local copies, waits for them, and re-layouts  6.47 us (5%)
    pallas_call x1, Pallas kernels, shards(): pl.pallas_call(functools.partial(kernel, ny, di, dt), out_shape=(jax.Shap...  131 us
    unnamed x11, local copies, waits for them, and re-layouts  5.68 us

profile of v1, /device:TPU:1, one launch (start us, length us, event | category | flops | bytes accessed | tf_op | source)
XLA Modules:
  0.0 139.2 jit_solution(15873767688302041223)
XLA Ops:
  1.3 0.0 copy-start
  1.3 1.0 copy-done
  2.3 0.0 copy-start.1
  2.3 1.0 copy-done.1
  3.2 0.0 copy-start.2
  3.2 0.9 copy-done.2
  4.2 0.0 copy-start.3
  4.2 0.9 copy-done.3
  5.1 131.4 %shard_map.84 = (f32[10,128]{1,0:T(8,128)S(1)}, f32[8,128]{1,0:T(8,128)S(1)}, f32[128,320]{1,0:T(8,128)S(1)}, f32[128,256]{1,0:T(8,128)S(1)}) custom-call(f32[1]{0:T(128)S(6)} %copy.13.scale_ref, bf16[128,1280]{1,0:T(8,128)(2,1)S(1)} %copy-done, bf16[128,1024]{1,0:T(8,128)(2,1)S(1)} %copy-done.2, bf16[1280,128]{1,0:T(8,128)(2,1)S(1)} %copy-done.1, ...), custom_call_target="tpu_custom_call" | custom-call | tf_op jit(solution)/shard_map/pallas_call | solution.py:644
  136.5 0.8 copy.9
  137.3 0.6 copy.14
  137.9 0.6 copy.15
  138.5 0.7 copy.16
Async XLA Ops:
  1.3 1.0 copy-start
  2.3 1.0 copy-start.1
  3.2 0.9 copy-start.2
  4.2 0.9 copy-start.3

commit v2 on v0

v2 whole, which is shorter than its diff:
```python
import functools

import jax
import jax.numpy as jnp
from jax import lax
from jax.experimental import pallas as pl
from jax.experimental.pallas import tpu as pltpu
from jax.sharding import PartitionSpec as P

Z = 16
XL = 2
T = 4
ROWS = 128
Q = 128
SUMS = 16
PIECE = ROWS + SUMS
eps = 1e-06
loss_factor = 256.0
f32 = jnp.float32
bf16 = jnp.bfloat16


def nt(left, right):
    return lax.dot_general(left, right, (((1,), (1,)), ((), ())), preferred_element_type=f32)


def tn(left, right):
    return lax.dot_general(left, right, (((0,), (0,)), ((), ())), preferred_element_type=f32)


def row_sums(values):
    return jnp.sum(jnp.transpose(values), axis=0, keepdims=True)


def as_columns(row):
    return jnp.transpose(jnp.broadcast_to(row, (ROWS, ROWS)))


def rows_of(*rows):
    index = lax.broadcasted_iota(jnp.int32, (8, rows[0].shape[1]), 0)
    out = jnp.zeros((8, rows[0].shape[1]), f32)
    for k, row in enumerate(rows):
        out = jnp.where(index == k, row, out)
    return out


def pack(values):
    high = values.astype(bf16)
    return jnp.concatenate([high, (values - high.astype(f32)).astype(bf16)], axis=0)


def unpack(parts):
    parts = parts.astype(f32)
    return parts[0:8] + parts[8:16]


def window_of(per):
    return max(-(-(((k * per) % 8) + per) // 8) * 8 for k in range(8))


def kernel(
    ny, di, dt,
    scale_ref, imgf_hbm, txtf_hbm, imgp_hbm, txtp_hbm,
    gip, gtp, gif, gtf,
    imgf, txtf, imgp, txtp,
    sqb, invr, own, img_all, zbuf, txt_all,
    psi, pst, gt_acc, col_acc,
    cs_send, cs_recv, rs_mid, rs_recv, gx_send, gx_recv, ga_send, ga_recv,
    gr_own, gr_all, yi_send, yi_recv, yt_send, yt_recv,
    xi_send, xi_recv, xt_send, xt_recv, zi_sum, zt_sum, zi_send, zi_recv, zt_send, zt_recv,
    in_ss, sq_ss, sq_rs, pp_ss, pp_rs, ig_ss, fw_ss, ig_rs, za_ss, za_rs,
    tx_ss, tx_rs, cs_ss, cs_rs, ri_ss, ri_rs, gx_ss, gx_rs, ga_ss, ga_rs,
    gr_ss, gr_rs, yi_ss, yi_rs, yt_ss, yt_rs, x_ss, x_rs, zi_ss, zi_rs, zt_ss, zt_rs,
):
    n_blocks = ny * XL
    n_plane = n_blocks * T
    n_half = n_plane // 2
    na = Z // T
    batch = ny * Z * XL * ROWS
    dp = lax.axis_index("dp")
    t = lax.axis_index("tensor")
    core = t % 2
    xl = dp % XL
    z = (dp // XL) % Z
    y = dp // (XL * Z)
    b = y * XL + xl
    p = b * T + t
    h = p // 2
    a = z // T
    c = z % T

    def plane_dev(q):
        block = q // T
        return (((block // XL) * Z + z) * XL + block % XL, q % T)

    def zt_dev(other, tensor):
        return ((y * Z + other) * XL + xl, tensor)

    def z_dev(other):
        return zt_dev(other, t)

    def y_dev(other):
        return ((other * Z + z) * XL + xl, t)

    def t_dev(other):
        return (dp, other)

    sibling = (dp, t + 1 - 2 * core)

    def remote(src, dst, send, recv, dev):
        return pltpu.make_async_remote_copy(
            src_ref=src, dst_ref=dst, send_sem=send, recv_sem=recv,
            device_id=dev, device_id_type=pl.DeviceIdType.MESH,
        )

    barrier = pltpu.get_barrier_semaphore()

    def greet(dev):
        pl.semaphore_signal(barrier, inc=1, device_id=dev, device_id_type=pl.DeviceIdType.MESH)

    @pl.loop(1, Z)
    def _(i):
        greet(z_dev((z + i) % Z))

    loads = [
        pltpu.make_async_copy(src, dst, in_ss.at[k])
        for k, (src, dst) in enumerate(
            [(imgf_hbm, imgf), (imgp_hbm, imgp), (txtf_hbm, txtf), (txtp_hbm, txtp)]
        )
    ]
    for copy in loads:
        copy.start()

    for e in (1, 2, Z - 1, Z - 2):
        for i in range(1, T):
            greet(zt_dev((z + e) % Z, (t + i) % T))

    @pl.loop(1, n_plane)
    def _(i):
        greet(plane_dev((p + i) % n_plane))

    scale = scale_ref[0]
    coef = scale * (loss_factor / (2.0 * batch))

    loads[0].wait()
    loads[1].wait()
    raw_img = jnp.dot(imgf[...], imgp[...], preferred_element_type=f32)
    loads[2].wait()
    loads[3].wait()
    raw_txt = jnp.dot(txtf[...], txtp[...], preferred_element_type=f32)
    sqb[t] = rows_of(row_sums(raw_img * raw_img), row_sums(raw_txt * raw_txt))
    pl.semaphore_wait(barrier, n_plane - 1 + Z - 1 + 4 * (T - 1))

    def sq_copy(i):
        return remote(sqb.at[t], sqb.at[t], sq_ss.at[i - 1], sq_rs.at[t], t_dev((t + i) % T))

    for i in range(1, T):
        sq_copy(i).start()
    for i in range(1, T):
        src = (t + i) % T
        remote(sqb.at[src], sqb.at[src], sq_ss.at[i - 1], sq_rs.at[src], t_dev(src)).wait_recv()
    square = (sqb[0] + sqb[1]) + (sqb[2] + sqb[3])
    inv = lax.rsqrt(square + eps)
    invr[...] = inv
    emb_txt = (raw_txt * as_columns(inv[1:2])).astype(bf16)
    own[1] = emb_txt
    zbuf[a] = emb_txt

    def img_slot(q):
        return img_all.at[
            pl.ds(pl.multiple_of((q // T) * ROWS, ROWS), ROWS),
            pl.ds(pl.multiple_of((q % T) * Q, Q), Q),
        ]

    def txt_slot(k, quarter):
        return txt_all.at[
            pl.ds(pl.multiple_of(k * ROWS, ROWS), ROWS),
            pl.ds(pl.multiple_of(quarter * Q, Q), Q),
        ]

    def za_copy(o):
        return remote(zbuf.at[a], zbuf.at[a], za_ss.at[o], za_rs.at[a], z_dev((z + T * o) % Z))

    def za_land(o):
        src = (a + o) % na
        return remote(zbuf.at[src], zbuf.at[src], za_ss.at[o], za_rs.at[src], z_dev((z + T * o) % Z))

    two = 2 - 4 * core

    def tx_copy(k, m):
        delta = (0, 1, two, -1)[m]
        return remote(
            zbuf.at[k], txt_slot(k, t), tx_ss.at[k * T + m], tx_rs.at[k * T + t],
            zt_dev((z - delta + Z) % Z, c),
        )

    def tx_local(k):
        return pltpu.make_async_copy(zbuf.at[k], txt_slot(k, t), tx_ss.at[k * T])

    def pass_on(k):
        for m in range(1, T):
            tx_copy(k, m).start()

        @pl.when(c != t)
        def _():
            tx_copy(k, 0).start()

        @pl.when(c == t)
        def _():
            tx_local(k).start()

    far_first = sorted(range(1, na), key=lambda o: -min(o, na - o))
    for o in far_first:
        za_copy(o).start()
    pass_on(a)

    emb_img = (raw_img * as_columns(inv[0:1])).astype(bf16)
    own[0] = emb_img
    own_img_copy = pltpu.make_async_copy(own.at[0], img_slot(p), in_ss.at[0])
    own_img_copy.start()

    def same_core(i):
        return ((h + i) % n_half) * 2 + core

    def ig_copy(i):
        return remote(own.at[0], img_slot(p), ig_ss.at[i], ig_rs.at[p], plane_dev(same_core(i)))

    def ig_land(i):
        q = same_core(i)
        return remote(own.at[0], img_slot(q), ig_ss.at[i], ig_rs.at[q], plane_dev(q))

    def fw_copy(i):
        q = same_core(i)
        return remote(img_slot(q), img_slot(q), fw_ss.at[i], ig_rs.at[q], sibling)

    def fw_land(i):
        q = ((h + i) % n_half) * 2 + 1 - core
        return remote(img_slot(q), img_slot(q), fw_ss.at[i], ig_rs.at[q], sibling)

    fw_own = remote(own.at[0], img_slot(p), fw_ss.at[0], ig_rs.at[p], sibling)

    @pl.loop(1, n_half)
    def _(i):
        ig_copy(i).start()

    fw_own.start()

    near_first = far_first[::-1]
    for o in [o for o in near_first if min(o, na - o) == 1]:
        za_land(o).wait_recv()
        pass_on((a + o) % na)

    @pl.loop(1, n_half)
    def _(i):
        ig_land(i).wait_recv()
        fw_copy(i).start()

    for o in [o for o in near_first if min(o, na - o) > 1]:
        za_land(o).wait_recv()
        pass_on((a + o) % na)

    own_img_copy.wait()

    @pl.loop(0, n_half)
    def _(i):
        fw_land(i).wait_recv()

    @pl.when(c == t)
    def _():
        for k in range(na):
            tx_local(k).wait()

    mine = (t - c + T) % T

    @pl.loop(0, na)
    def _(k):
        for quarter in range(T):
            @pl.when((mine != 0) | (t != quarter))
            def _(quarter=quarter):
                remote(
                    zbuf.at[0], txt_slot(k, quarter), tx_ss.at[0],
                    tx_rs.at[k * T + quarter], sibling,
                ).wait_recv()

    keys = na * ROWS
    gt_acc[...] = jnp.zeros_like(gt_acc)
    col_acc[...] = jnp.zeros_like(col_acc)

    def fold(values):
        return sum(values[:, k * ROWS:(k + 1) * ROWS] for k in range(keys // ROWS))

    def cs_copy(block):
        return remote(
            cs_send.at[pl.ds((1 - core) * n_half + block * 2, 2)],
            cs_recv.at[pl.ds(block * 2, 2)], cs_ss.at[block], cs_rs.at[block], sibling,
        )

    def rs_copy(k):
        return remote(
            rs_mid.at[k], rs_recv.at[h], ri_ss.at[k], ri_rs.at[h], plane_dev(k * 2 + core)
        )

    def both_cores(block):
        cs_copy(block).wait_recv()
        for part in range(2):
            k = block * 2 + part
            one = cs_send.at[core * n_half + k]
            other = cs_recv.at[k]
            rs_mid[k, 0:ROWS, :] = (
                one[0:ROWS, :].astype(f32) + other[0:ROWS, :].astype(f32)
            ).astype(bf16)
            rs_mid[k, ROWS:PIECE, :] = pack(unpack(one[ROWS:PIECE, :]) + unpack(other[ROWS:PIECE, :]))

            @pl.when(k != h)
            def _(k=k):
                rs_copy(k).start()

    @pl.loop(0, n_blocks)
    def _(n):
        block = (b + 1 + n) % n_blocks
        rows = img_all[pl.ds(pl.multiple_of(block * ROWS, ROWS), ROWS), :]
        cos = nt(rows, txt_all[...])
        expo = jnp.exp(scale * (cos - 1.0))
        i = lax.broadcasted_iota(jnp.int32, (ROWS, keys), 0)
        j = lax.broadcasted_iota(jnp.int32, (ROWS, keys), 1)
        mask = (j - i) == jnp.where((block == b) & (t == c), a * ROWS, -2 * ROWS)
        weights = jnp.where(mask, 0.0, expo).astype(bf16)
        off = weights.astype(f32)
        inner = off * cos
        diag = jnp.sum(jnp.where(mask, expo, 0.0), axis=0, keepdims=True)
        match = jnp.sum(jnp.where(mask, cos, 0.0), axis=0, keepdims=True)
        sums = pack(
            rows_of(row_sums(fold(off)), fold(diag), row_sums(fold(inner)), fold(match))
        )
        col_acc[...] += rows_of(
            jnp.sum(off, axis=0, keepdims=True), diag,
            jnp.sum(inner, axis=0, keepdims=True), match,
        )
        part = jnp.dot(weights, txt_all[...], preferred_element_type=f32)
        for quarter in range(T):
            k = (quarter % 2) * n_half + block * 2 + quarter // 2
            cs_send[k, 0:ROWS, :] = part[:, quarter * Q:(quarter + 1) * Q].astype(bf16)
            cs_send[k, ROWS:PIECE, :] = sums
        cs_copy(block).start()
        gt_acc[...] += tn(weights, rows)

    def gx_copy(k, quarter):
        delta = jnp.where(
            mine == 0, 0, jnp.where(mine == 1, 1, jnp.where(mine == 3, -1, 2 - 4 * (quarter % 2)))
        )
        return remote(
            gx_send.at[k * T + quarter], gx_recv.at[k * T + mine], gx_ss.at[k * T + quarter],
            gx_rs.at[k * T + mine], zt_dev((z + delta + Z) % Z, quarter),
        )

    for k in range(na):
        sums = pack(col_acc[:, k * ROWS:(k + 1) * ROWS])
        for quarter in range(T):
            slot = k * T + quarter
            gx_send[slot, 0:ROWS, :] = gt_acc[
                k * ROWS:(k + 1) * ROWS, quarter * Q:(quarter + 1) * Q
            ].astype(bf16)
            gx_send[slot, ROWS:PIECE, :] = sums

    @pl.loop(0, na)
    def _(n):
        k = (a + na // 2 + n) % na
        for quarter in range(T):
            @pl.when((mine != 0) | (t != quarter))
            def _(quarter=quarter):
                gx_copy(k, quarter).start()

    @pl.loop(0, n_blocks)
    def _(n):
        both_cores((b + 1 + n) % n_blocks)

    def ga_copy(o):
        return remote(
            ga_send.at[o], ga_recv.at[a], ga_ss.at[o], ga_rs.at[a], z_dev((z + T * o) % Z)
        )

    def near_sum(o):
        k = (a + o) % na

        @pl.when(c == t)
        def _():
            gx_recv[k * T] = gx_send[k * T + t]

        for m in range(T):
            wait = remote(
                gx_send.at[0], gx_recv.at[k * T + m], gx_ss.at[0], gx_rs.at[k * T + m], sibling
            ).wait_recv
            if m == 0:
                pl.when(c != t)(wait)
            else:
                wait()
        total = sum(gx_recv[k * T + m, 0:ROWS, :].astype(f32) for m in range(T))
        ga_send[o, 0:ROWS, :] = total.astype(bf16)
        ga_send[o, ROWS:PIECE, :] = pack(
            sum(unpack(gx_recv[k * T + m, ROWS:PIECE, :]) for m in range(T))
        )

    for o in far_first:
        near_sum(o)
        ga_copy(o).start()
    near_sum(0)

    def raw_grad(total, sums, emb, target, inv_row):
        off, diag, inner, match = (sums[k:k + 1] for k in range(4))
        factor = coef / (off + diag) * inv_row
        align = inner - off * match
        return (
            as_columns(factor) * (total - as_columns(off) * target - as_columns(align) * emb)
        ).astype(bf16)

    def gr_copy(m, i):
        return remote(
            gr_own.at[m], gr_all.at[m, :, pl.ds(pl.multiple_of(t * Q, Q), Q)],
            gr_ss.at[m * T + i], gr_rs.at[m * T + t], t_dev((t + i) % T),
        )

    own_gr = [
        pltpu.make_async_copy(
            gr_own.at[m], gr_all.at[m, :, pl.ds(pl.multiple_of(t * Q, Q), Q)], gr_ss.at[m * T]
        )
        for m in range(2)
    ]

    diy, dty = di // ny, dt // ny
    per_i, per_t = diy // (Z * XL), dty // (Z * XL)
    win = window_of(per_i)

    class Proj:
        def __init__(self, feat, per_y, send, recv, ss, rs, x_send, x_recv, x_sem, zsum, m):
            self.__dict__.update(locals())

        def y_copy(self, i):
            dst = (y + i) % ny
            return remote(
                self.send.at[pl.ds(pl.multiple_of(dst * self.per_y, 16), self.per_y)],
                self.recv.at[y], self.ss.at[i], self.rs.at[y], y_dev(dst),
            )

        def x_copy(self):
            return remote(
                self.x_send, self.x_recv, x_ss.at[self.x_sem], x_rs.at[self.x_sem],
                (dp - xl + (XL - 1 - xl), t),
            )

        def begin(self, grad):
            gr_own[self.m] = grad
            for k in range(0, self.feat.shape[1], 128):
                self.send[k:k + 128, :] = tn(self.feat[:, k:k + 128], grad).astype(bf16)
            for i in range(1, ny):
                self.y_copy(i).start()

        def middle(self):
            self.zsum[...] = self.send[
                pl.ds(pl.multiple_of(y * self.per_y, 16), self.per_y), :
            ].astype(f32)
            for i in range(1, ny):
                src = (y + i) % ny
                remote(
                    self.send.at[pl.ds(0, self.per_y)], self.recv.at[src], self.ss.at[i],
                    self.rs.at[src], y_dev(src),
                ).wait_recv()
            total = self.zsum[...]
            for i in range(1, ny):
                total += self.recv[(y + i) % ny].astype(f32)
            self.zsum[...] = total
            if XL == 2:
                self.x_send[...] = total.astype(bf16)
                self.x_copy().start()

        def last(self):
            if XL == 2:
                self.x_copy().wait_recv()
                self.zsum[...] += self.x_recv[...].astype(f32)

        def finish(self):
            for i in range(1, ny):
                self.y_copy(i).wait_send()
            if XL == 2:
                self.x_copy().wait_send()

    img = Proj(imgf, diy, yi_send, yi_recv, yi_ss, yi_rs, xi_send, xi_recv, 0, zi_sum, 0)
    txt = Proj(txtf, dty, yt_send, yt_recv, yt_ss, yt_rs, xt_send, xt_recv, 1, zt_sum, 1)

    def rs_sum(i, carry):
        total, sums = carry
        src = (h + i) % n_half
        remote(
            rs_mid.at[0], rs_recv.at[src], ri_ss.at[0], ri_rs.at[src], sibling
        ).wait_recv()
        return (
            total + rs_recv[src, 0:ROWS, :].astype(f32),
            sums + unpack(rs_recv[src, ROWS:PIECE, :]),
        )

    total_img, sums_img = lax.fori_loop(
        1, n_half, rs_sum, (rs_mid[h, 0:ROWS, :].astype(f32), unpack(rs_mid[h, ROWS:PIECE, :]))
    )
    own_img = own[0].astype(f32)
    own_txt = own[1].astype(f32)
    img.begin(raw_grad(total_img, sums_img, own_img, own_txt, invr[0:1, :]))

    total_txt = ga_send[0, 0:ROWS, :].astype(f32)
    sums_txt = unpack(ga_send[0, ROWS:PIECE, :])
    for o in near_first:
        src = (a + o) % na
        remote(ga_send.at[0], ga_recv.at[src], ga_ss.at[o], ga_rs.at[src], sibling).wait_recv()
        total_txt += ga_recv[src, 0:ROWS, :].astype(f32)
        sums_txt += unpack(ga_recv[src, ROWS:PIECE, :])
    txt.begin(raw_grad(total_txt, sums_txt, own_txt, own_img, invr[1:2, :]))

    img.middle()
    txt.middle()

    for m in range(2):
        own_gr[m].start()
        for i in range(1, T):
            gr_copy(m, i).start()
    di4, dt4 = di // T, dt // T

    def pp_pair(i, src, first):
        other = (t + i) % T
        quarter = pl.ds(pl.multiple_of(src * Q, Q), Q)
        return (
            remote(
                imgp.at[pl.ds(pl.multiple_of(first * di4, 16), di4), :], psi.at[:, quarter],
                pp_ss.at[2 * i], pp_rs.at[2 * src], t_dev(other),
            ),
            remote(
                txtp.at[pl.ds(pl.multiple_of(first * dt4, 16), dt4), :], pst.at[:, quarter],
                pp_ss.at[2 * i + 1], pp_rs.at[2 * src + 1], t_dev(other),
            ),
        )

    def pp_copies(i):
        return pp_pair(i, t, (t + i) % T)

    for i in range(1, T):
        for copy in pp_copies(i):
            copy.start()
    own_pp = [
        pltpu.make_async_copy(
            ref.at[pl.ds(pl.multiple_of(t * size, 16), size), :],
            dst.at[:, pl.ds(pl.multiple_of(t * Q, Q), Q)], pp_ss.at[k],
        )
        for k, (ref, dst, size) in enumerate([(imgp, psi, di4), (txtp, pst, dt4)])
    ]
    for copy in own_pp:
        copy.start()

    def zi_copy(i):
        dst = (z + i) % Z
        return remote(zi_send.at[dst], zi_recv.at[z], zi_ss.at[i], zi_rs.at[z], z_dev(dst))

    def zt_copy(i):
        dst = (z + i) % Z
        return remote(zt_send.at[dst], zt_recv.at[z], zt_ss.at[i], zt_rs.at[z], z_dev(dst))

    img.last()

    @pl.loop(0, Z)
    def _(n):
        i = (Z // 2 + n) % Z
        dst = (z + i) % Z
        first = ((dst * XL + xl) * per_i) // 8 * 8
        zi_send[dst] = zi_sum[pl.ds(pl.multiple_of(first, 8), win), :].astype(bf16)

        @pl.when(i > 0)
        def _():
            zi_copy(i).start()

    txt.last()

    @pl.loop(0, Z)
    def _(n):
        i = (Z // 2 + n) % Z
        dst = (z + i) % Z
        first = (dst * XL + xl) * per_t
        block = zt_sum[pl.ds(pl.multiple_of(first, 8), per_t), :]
        if per_t % 16:
            block = jnp.concatenate([block, block], axis=0)
        zt_send[dst] = block.astype(bf16)

        @pl.when(i > 0)
        def _():
            zt_copy(i).start()

    for m in range(2):
        own_gr[m].wait()
        own_pp[m].wait()
        for i in range(1, T):
            src = (t + i) % T
            remote(
                gr_own.at[m], gr_all.at[m, :, pl.ds(pl.multiple_of(src * Q, Q), Q)],
                gr_ss.at[m * T + i], gr_rs.at[m * T + src], t_dev(src),
            ).wait_recv()
    for i in range(1, T):
        for copy in pp_pair(i, (t + i) % T, 0):
            copy.wait_recv()
    gif[...] = nt(gr_all[0], psi[...])
    gtf[...] = nt(gr_all[1], pst[...])

    def zi_add(i, total):
        src = (z + i) % Z
        remote(zi_send.at[0], zi_recv.at[src], zi_ss.at[i], zi_rs.at[src], sibling).wait_recv()
        return total + zi_recv[src].astype(f32)

    total = lax.fori_loop(1, Z, zi_add, zi_send[z].astype(f32))
    shift = ((z * XL + xl) * per_i) % 8
    result = total[0:per_i]
    for k in sorted({(k * per_i) % 8 for k in range(8)} - {0}):
        result = jnp.where(shift == k, total[k:k + per_i], result)
    gip[...] = result

    def zt_add(i, total):
        src = (z + i) % Z
        remote(zt_send.at[0], zt_recv.at[src], zt_ss.at[i], zt_rs.at[src], sibling).wait_recv()
        return total + zt_recv[src, 0:per_t, :].astype(f32)

    gtp[...] = lax.fori_loop(1, Z, zt_add, zt_send[z, 0:per_t, :].astype(f32))

    for i in range(1, T):
        sq_copy(i).wait_send()
        for copy in pp_copies(i):
            copy.wait_send()
        for m in range(2):
            gr_copy(m, i).wait_send()
    for o in far_first:
        za_copy(o).wait_send()
        ga_copy(o).wait_send()
    fw_own.wait_send()

    @pl.loop(1, n_half)
    def _(i):
        ig_copy(i).wait_send()
        fw_copy(i).wait_send()
        rs_copy((h + i) % n_half).wait_send()

    @pl.loop(0, n_blocks)
    def _(block):
        cs_copy(block).wait_send()

    @pl.loop(0, na)
    def _(k):
        for m in range(1, T):
            tx_copy(k, m).wait_send()

        @pl.when(c != t)
        def _():
            tx_copy(k, 0).wait_send()

        for quarter in range(T):
            @pl.when((mine != 0) | (t != quarter))
            def _(quarter=quarter):
                gx_copy(k, quarter).wait_send()

    img.finish()
    txt.finish()

    @pl.loop(1, Z)
    def _(i):
        zi_copy(i).wait_send()
        zt_copy(i).wait_send()


def shards(ny, img_feat, txt_feat, img_proj, txt_proj, logit_scale):
    di, dt = img_feat.shape[1], txt_feat.shape[1]
    n_blocks = ny * XL
    n_plane = n_blocks * T
    n_half = n_plane // 2
    na = Z // T
    keys = na * ROWS
    emb = T * Q
    ndp = ny * Z * XL
    diy, dty = di // ny, dt // ny
    win = window_of(diy // (Z * XL))
    tall = max(dty // (Z * XL), 16)
    dma = pltpu.SemaphoreType.DMA
    vmem = pltpu.VMEM
    piece = (PIECE, Q)
    scratch = [
        vmem((ROWS, di), bf16),
        vmem((ROWS, dt), bf16),
        vmem((di, Q), bf16),
        vmem((dt, Q), bf16),
        vmem((T, 8, ROWS), f32),
        vmem((8, ROWS), f32),
        vmem((2, ROWS, Q), bf16),
        vmem((n_blocks * ROWS, emb), bf16),
        vmem((na, ROWS, Q), bf16),
        vmem((keys, emb), bf16),
        vmem((di // T, emb), bf16),
        vmem((dt // T, emb), bf16),
        vmem((keys, emb), f32),
        vmem((8, keys), f32),
        vmem((n_plane, *piece), bf16),
        vmem((n_half, *piece), bf16),
        vmem((n_half, *piece), bf16),
        vmem((n_half, *piece), bf16),
        vmem((na * T, *piece), bf16),
        vmem((na * T, *piece), bf16),
        vmem((na, *piece), bf16),
        vmem((na, *piece), bf16),
        vmem((2, ROWS, Q), bf16),
        vmem((2, ROWS, emb), bf16),
        vmem((di, Q), bf16),
        vmem((ny, diy, Q), bf16),
        vmem((dt, Q), bf16),
        vmem((ny, dty, Q), bf16),
        vmem((diy, Q), bf16),
        vmem((diy, Q), bf16),
        vmem((dty, Q), bf16),
        vmem((dty, Q), bf16),
        vmem((diy, Q), f32),
        vmem((dty, Q), f32),
        vmem((Z, win, Q), bf16),
        vmem((Z, win, Q), bf16),
        vmem((Z, tall, Q), bf16),
        vmem((Z, tall, Q), bf16),
    ]
    wide = max(ny, 2)
    sems = [
        4, T, T, 2 * T, 2 * T, n_half, n_half, n_plane, na, na,
        na * T, na * T, n_blocks, n_blocks, n_half, n_half, na * T, na * T, na, na,
        2 * T, 2 * T, wide, wide, wide, wide, 2, 2, Z, Z, Z, Z,
    ]
    scratch += [dma((n,)) for n in sems]
    whole = pl.BlockSpec(memory_space=pltpu.VMEM)
    return pl.pallas_call(
        functools.partial(kernel, ny, di, dt),
        out_shape=(
            jax.ShapeDtypeStruct((di // ndp, Q), f32),
            jax.ShapeDtypeStruct((dt // ndp, Q), f32),
            jax.ShapeDtypeStruct((ROWS, di // T), f32),
            jax.ShapeDtypeStruct((ROWS, dt // T), f32),
        ),
        in_specs=[pl.BlockSpec(memory_space=pltpu.SMEM)]
        + [pl.BlockSpec(memory_space=pl.ANY)] * 4,
        out_specs=(whole,) * 4,
        scratch_shapes=scratch,
        compiler_params=pltpu.CompilerParams(
            collective_id=0, has_side_effects=True, vmem_limit_bytes=56 * 1024 * 1024
        ),
    )(logit_scale, img_feat, txt_feat, img_proj, txt_proj)


def solution(mesh):
    ny = mesh.shape["dp"] // (Z * XL)
    return jax.shard_map(
        functools.partial(shards, ny),
        mesh=mesh,
        in_specs=(P("dp", None), P("dp", None), P(None, "tensor"), P(None, "tensor"), P()),
        out_specs=(P("dp", "tensor"), P("dp", "tensor"), P("dp", "tensor"), P("dp", "tensor")),
        check_vma=False,
    )
```

time: 2340 us -> 96.3 us (0.04)
  the two profiles are of different devices: /device:TPU:2 before, /device:TPU:1 now
where the time goes in v2:
time: 96.3 us; the launch traced here: 96.1 us
  Pallas kernels  91.1 us (95%)
  local copies, waits for them, and re-layouts  3.67 us (4%)
  between operations  1.31 us (1%)
    pallas_call x1, Pallas kernels, shards(): pl.pallas_call(functools.partial(kernel, ny, di, dt), out_shape=(jax.Shap...  91.1 us
    unnamed x9, local copies, waits for them, and re-layouts  1.93 us

profile of v2, /device:TPU:1, one launch (start us, length us, event | category | flops | bytes accessed | tf_op | source)
XLA Modules:
  0.0 96.1 jit_solution(14449709138567702428)
XLA Ops:
  1.3 91.1 %shard_map.84 = (f32[10,128]{1,0:T(8,128)}, f32[8,128]{1,0:T(8,128)}, f32[128,320]{1,0:T(8,128)}, f32[128,256]{1,0:T(8,128)}) custom-call(f32[1]{0:T(128)S(6)} %copy.13.scale_ref, bf16[128,1280]{1,0:T(8,128)(2,1)} %imgf_hbm.1, bf16[128,1024]{1,0:T(8,128)(2,1)} %txtf_hbm.1, bf16[1280,128]{1,0:T(8,128)(2,1)} %imgp_hbm.1, bf16[1024,128]{1,0:T(8,128)(2,1)} %txtp_hbm.1), custom_call_target="tpu_custom_call" | custom-call | tf_op jit(solution)/shard_map/pallas_call | solution.py:733
  92.4 0.0 copy-start.1
  92.4 0.0 copy-start
  92.4 1.7 %copy.9 = f32[128,320]{0,1:T(8,128)} copy(f32[128,320]{1,0:T(8,128)} %get-tuple-element.6) | data formatting | bytes 327680 | tf_op jit(solution)/shard_map/pallas_call | solution.py:733
  94.2 0.0 copy-done.1
  94.2 0.0 copy-start.2
  94.2 0.6 copy.14
  94.8 0.1 copy-done.2
  94.9 0.6 copy.15
  95.5 0.0 copy-done
  95.5 0.7 copy.16
Async XLA Ops:
  92.4 1.8 %copy-start.1 = (f32[10,128]{1,0:T(8,128)S(1)}, f32[10,128]{1,0:T(8,128)}, u32[]{:S(2)}) copy-start(f32[10,128]{1,0:T(8,128)} %get-tuple-element.12) | copy-start | bytes 15364
  92.4 3.0 %copy-start = (f32[128,256]{1,0:T(8,128)S(1)}, f32[128,256]{1,0:T(8,128)}, u32[]{:S(2)}) copy-start(f32[128,256]{1,0:T(8,128)} %get-tuple-element.15) | copy-start | bytes 393220
  94.2 0.7 copy-start.2

commit v3 on v2

--- a/solution.py
+++ b/solution.py
@@ -64,7 +64,7 @@
     gip, gtp, gif, gtf,
     imgf, txtf, imgp, txtp,
     sqb, invr, own, img_all, zbuf, txt_all,
-    psi, pst, gt_acc, col_acc,
+    psi, pst, gt_acc, col_acc, weight,
     cs_send, cs_recv, rs_mid, rs_recv, gx_send, gx_recv, ga_send, ga_recv,
     gr_own, gr_all, yi_send, yi_recv, yt_send, yt_recv,
     xi_send, xi_recv, xt_send, xt_recv, zi_sum, zt_sum, zi_send, zi_recv, zt_send, zt_recv,
@@ -86,6 +86,7 @@
     b = y * XL + xl
     p = b * T + t
     h = p // 2
+    xh = t // 2
     a = z // T
     c = z % T
 
@@ -219,22 +220,23 @@
     own_img_copy = pltpu.make_async_copy(own.at[0], img_slot(p), in_ss.at[0])
     own_img_copy.start()
 
-    def same_core(i):
-        return ((h + i) % n_half) * 2 + core
+    def peer(n, flip):
+        return ((b + n + n_blocks) % n_blocks) * 2 + xh + flip - 2 * xh * flip
 
     def ig_copy(i):
-        return remote(own.at[0], img_slot(p), ig_ss.at[i], ig_rs.at[p], plane_dev(same_core(i)))
+        dst = peer(-(i // 2), i % 2) * 2 + core
+        return remote(own.at[0], img_slot(p), ig_ss.at[i], ig_rs.at[p], plane_dev(dst))
 
     def ig_land(i):
-        q = same_core(i)
+        q = peer(i // 2, i % 2) * 2 + core
         return remote(own.at[0], img_slot(q), ig_ss.at[i], ig_rs.at[q], plane_dev(q))
 
     def fw_copy(i):
-        q = same_core(i)
+        q = peer(i // 2, i % 2) * 2 + core
         return remote(img_slot(q), img_slot(q), fw_ss.at[i], ig_rs.at[q], sibling)
 
     def fw_land(i):
-        q = ((h + i) % n_half) * 2 + 1 - core
+        q = peer(i // 2, i % 2) * 2 + 1 - core
         return remote(img_slot(q), img_slot(q), fw_ss.at[i], ig_rs.at[q], sibling)
 
     fw_own = remote(own.at[0], img_slot(p), fw_ss.at[0], ig_rs.at[p], sibling)
@@ -244,36 +246,25 @@
         ig_copy(i).start()
 
     fw_own.start()
-
     near_first = far_first[::-1]
-    for o in [o for o in near_first if min(o, na - o) == 1]:
-        za_land(o).wait_recv()
-        pass_on((a + o) % na)
-
-    @pl.loop(1, n_half)
-    def _(i):
-        ig_land(i).wait_recv()
-        fw_copy(i).start()
-
-    for o in [o for o in near_first if min(o, na - o) > 1]:
-        za_land(o).wait_recv()
-        pass_on((a + o) % na)
-
-    own_img_copy.wait()
-
-    @pl.loop(0, n_half)
-    def _(i):
-        fw_land(i).wait_recv()
-
-    @pl.when(c == t)
-    def _():
-        for k in range(na):
-            tx_local(k).wait()
+    near_groups = [o for o in near_first if min(o, na - o) == 1]
+    far_groups = [o for o in near_first if min(o, na - o) > 1]
 
     mine = (t - c + T) % T
 
-    @pl.loop(0, na)
-    def _(k):
+    def delta_of(quarter):
+        return jnp.where(
+            mine == 0, 0, jnp.where(mine == 1, 1, jnp.where(mine == 3, -1, 2 - 4 * (quarter % 2)))
+        )
+
+    base = jnp.where(mine == 2, a, ((z + delta_of(0) + Z) % Z) // T)
+    turn = jnp.where((mine == 2) & (c < T // 2), -1, 1)
+    if na == 4:
+        order = [base, (base + turn + na) % na, (base - turn + na) % na, (base + 2) % na]
+    else:
+        order = [(base + n) % na for n in range(na)]
+
+    def keys_ready(k):
         for quarter in range(T):
             @pl.when((mine != 0) | (t != quarter))
             def _(quarter=quarter):
@@ -282,12 +273,83 @@
                     tx_rs.at[k * T + quarter], sibling,
                 ).wait_recv()
 
+        @pl.when(c == t)
+        def _():
+            tx_local(k).wait()
+
     keys = na * ROWS
-    gt_acc[...] = jnp.zeros_like(gt_acc)
     col_acc[...] = jnp.zeros_like(col_acc)
 
     def fold(values):
-        return sum(values[:, k * ROWS:(k + 1) * ROWS] for k in range(keys // ROWS))
+        return sum(values[:, k * ROWS:(k + 1) * ROWS] for k in range(values.shape[1] // ROWS))
+
+    def score(first, count, k):
+        rows = img_all[pl.ds(pl.multiple_of(first, ROWS), count), :]
+        cos = nt(rows, txt_all[pl.ds(pl.multiple_of(k * ROWS, ROWS), ROWS), :])
+        expo = jnp.exp(scale * (cos - 1.0))
+        i = lax.broadcasted_iota(jnp.int32, (count, ROWS), 0)
+        j = lax.broadcasted_iota(jnp.int32, (count, ROWS), 1)
+        mask = (j - i) == jnp.where((k == a) & (t == c), first - b * ROWS, ROWS)
+        part = jnp.where(mask, 0.0, expo).astype(bf16)
+        weight[
+            pl.ds(pl.multiple_of(first, ROWS), count), pl.ds(pl.multiple_of(k * ROWS, ROWS), ROWS)
+        ] = part
+        none = jnp.zeros((1, ROWS), f32)
+        col_acc[k] += rows_of(
+            jnp.sum(part.astype(f32), axis=0, keepdims=True),
+            jnp.sum(jnp.where(mask, expo, 0.0), axis=0, keepdims=True),
+            none,
+            jnp.sum(jnp.where(mask, cos, 0.0), axis=0, keepdims=True),
+        )
+        gt_acc[...] += tn(part, rows)
+
+    def gx_copy(k, quarter):
+        return remote(
+            gx_send.at[k * T + quarter], gx_recv.at[k * T + mine], gx_ss.at[k * T + quarter],
+            gx_rs.at[k * T + mine], zt_dev((z + delta_of(quarter) + Z) % Z, quarter),
+        )
+
+    def texts_out(k):
+        total = gt_acc[...]
+        rows = txt_all[pl.ds(pl.multiple_of(k * ROWS, ROWS), ROWS), :].astype(f32)
+        none = jnp.zeros((1, ROWS), f32)
+        sums = pack(col_acc[k] + rows_of(none, none, row_sums(fold(total * rows))))
+        for quarter in range(T):
+            gx_send[k * T + quarter, 0:ROWS, :] = total[:, quarter * Q:(quarter + 1) * Q].astype(bf16)
+            gx_send[k * T + quarter, ROWS:PIECE, :] = sums
+
+            @pl.when((mine != 0) | (t != quarter))
+            def _(quarter=quarter):
+                gx_copy(k, quarter).start()
+
+    for o in near_groups:
+        za_land(o).wait_recv()
+        pass_on((a + o) % na)
+
+    @pl.loop(1, n_half)
+    def _(i):
+        ig_land(i).wait_recv()
+        fw_copy(i).start()
+
+    for o in far_groups:
+        za_land(o).wait_recv()
+        pass_on((a + o) % na)
+    own_img_copy.wait()
+
+    @pl.loop(0, n_half)
+    def _(i):
+        fw_land(i).wait_recv()
+
+    tall_rows = min(4, n_blocks) * ROWS
+    for k in order:
+        keys_ready(k)
+        gt_acc[...] = jnp.zeros_like(gt_acc)
+
+        @pl.loop(0, n_blocks * ROWS // tall_rows)
+        def _(n, k=k):
+            score(n * tall_rows, tall_rows, k)
+
+        texts_out(k)
 
     def cs_copy(block):
         return remote(
@@ -318,61 +380,20 @@
     @pl.loop(0, n_blocks)
     def _(n):
         block = (b + 1 + n) % n_blocks
-        rows = img_all[pl.ds(pl.multiple_of(block * ROWS, ROWS), ROWS), :]
-        cos = nt(rows, txt_all[...])
-        expo = jnp.exp(scale * (cos - 1.0))
-        i = lax.broadcasted_iota(jnp.int32, (ROWS, keys), 0)
-        j = lax.broadcasted_iota(jnp.int32, (ROWS, keys), 1)
-        mask = (j - i) == jnp.where((block == b) & (t == c), a * ROWS, -2 * ROWS)
-        weights = jnp.where(mask, 0.0, expo).astype(bf16)
-        off = weights.astype(f32)
-        inner = off * cos
-        diag = jnp.sum(jnp.where(mask, expo, 0.0), axis=0, keepdims=True)
-        match = jnp.sum(jnp.where(mask, cos, 0.0), axis=0, keepdims=True)
+        first = pl.ds(pl.multiple_of(block * ROWS, ROWS), ROWS)
+        part = jnp.dot(weight[first, :], txt_all[...], preferred_element_type=f32)
+        diag = jnp.where(block == b, col_acc[a], 0.0)
         sums = pack(
-            rows_of(row_sums(fold(off)), fold(diag), row_sums(fold(inner)), fold(match))
-        )
-        col_acc[...] += rows_of(
-            jnp.sum(off, axis=0, keepdims=True), diag,
-            jnp.sum(inner, axis=0, keepdims=True), match,
-        )
-        part = jnp.dot(weights, txt_all[...], preferred_element_type=f32)
+            rows_of(
+                row_sums(fold(weight[first, :].astype(f32))), diag[1:2],
+                row_sums(fold(part * img_all[first, :].astype(f32))), diag[3:4],
+            )
+        )
         for quarter in range(T):
             k = (quarter % 2) * n_half + block * 2 + quarter // 2
             cs_send[k, 0:ROWS, :] = part[:, quarter * Q:(quarter + 1) * Q].astype(bf16)
             cs_send[k, ROWS:PIECE, :] = sums
         cs_copy(block).start()
-        gt_acc[...] += tn(weights, rows)
-
-    def gx_copy(k, quarter):
-        delta = jnp.where(
-            mine == 0, 0, jnp.where(mine == 1, 1, jnp.where(mine == 3, -1, 2 - 4 * (quarter % 2)))
-        )
-        return remote(
-            gx_send.at[k * T + quarter], gx_recv.at[k * T + mine], gx_ss.at[k * T + quarter],
-            gx_rs.at[k * T + mine], zt_dev((z + delta + Z) % Z, quarter),
-        )
-
-    for k in range(na):
-        sums = pack(col_acc[:, k * ROWS:(k + 1) * ROWS])
-        for quarter in range(T):
-            slot = k * T + quarter
-            gx_send[slot, 0:ROWS, :] = gt_acc[
-                k * ROWS:(k + 1) * ROWS, quarter * Q:(quarter + 1) * Q
-            ].astype(bf16)
-            gx_send[slot, ROWS:PIECE, :] = sums
-
-    @pl.loop(0, na)
-    def _(n):
-        k = (a + na // 2 + n) % na
-        for quarter in range(T):
-            @pl.when((mine != 0) | (t != quarter))
-            def _(quarter=quarter):
-                gx_copy(k, quarter).start()
-
-    @pl.loop(0, n_blocks)
-    def _(n):
-        both_cores((b + 1 + n) % n_blocks)
 
     def ga_copy(o):
         return remote(
@@ -400,7 +421,15 @@
             sum(unpack(gx_recv[k * T + m, ROWS:PIECE, :]) for m in range(T))
         )
 
-    for o in far_first:
+    for o in near_groups:
+        near_sum(o)
+        ga_copy(o).start()
+
+    @pl.loop(0, n_blocks)
+    def _(n):
+        both_cores((b + 1 + n) % n_blocks)
+
+    for o in far_groups:
         near_sum(o)
         ga_copy(o).start()
     near_sum(0)
@@ -695,8 +724,9 @@
         vmem((keys, emb), bf16),
         vmem((di // T, emb), bf16),
         vmem((dt // T, emb), bf16),
-        vmem((keys, emb), f32),
-        vmem((8, keys), f32),
+        vmem((ROWS, emb), f32),
+        vmem((na, 8, ROWS), f32),
+        vmem((n_blocks * ROWS, keys), bf16),
         vmem((n_plane, *piece), bf16),
         vmem((n_half, *piece), bf16),
         vmem((n_half, *piece), bf16),

time: 96.3 us -> 90 us (0.935)
  Pallas kernels: 91.1 us -> 84.8 us
    pallas_call x1, Pallas kernels: 91.1 us -> 84.8 us  [shards(): pl.pallas_call(functools.partial(kernel, ny, di, dt), out_shape=(jax.Shap...]
where the time goes in v3:
time: 90 us; the launch traced here: 89.8 us
  Pallas kernels  84.8 us (94%)
  local copies, waits for them, and re-layouts  3.67 us (4%)
  between operations  1.31 us (1%)
    pallas_call x1, Pallas kernels, shards(): pl.pallas_call(functools.partial(kernel, ny, di, dt), out_shape=(jax.Shap...  84.8 us
    unnamed x9, local copies, waits for them, and re-layouts  1.93 us

profile of v3, /device:TPU:1, one launch (start us, length us, event | category | flops | bytes accessed | tf_op | source)
XLA Modules:
  0.0 89.8 jit_solution(8169176775795005003)
XLA Ops:
  1.3 84.8 %shard_map.84 = (f32[10,128]{1,0:T(8,128)}, f32[8,128]{1,0:T(8,128)}, f32[128,320]{1,0:T(8,128)}, f32[128,256]{1,0:T(8,128)}) custom-call(f32[1]{0:T(128)S(6)} %copy.13.scale_ref, bf16[128,1280]{1,0:T(8,128)(2,1)} %imgf_hbm.1, bf16[128,1024]{1,0:T(8,128)(2,1)} %txtf_hbm.1, bf16[1280,128]{1,0:T(8,128)(2,1)} %imgp_hbm.1, bf16[1024,128]{1,0:T(8,128)(2,1)} %txtp_hbm.1), custom_call_target="tpu_custom_call" | custom-call | tf_op jit(solution)/shard_map/pallas_call | solution.py:763
  86.1 0.0 copy-start.1
  86.1 0.0 copy-start
  86.1 1.7 %copy.9 = f32[128,320]{0,1:T(8,128)} copy(f32[128,320]{1,0:T(8,128)} %get-tuple-element.6) | data formatting | bytes 327680 | tf_op jit(solution)/shard_map/pallas_call | solution.py:763
  87.9 0.0 copy-done.1
  87.9 0.0 copy-start.2
  87.9 0.6 copy.14
  88.5 0.1 copy-done.2
  88.5 0.6 copy.15
  89.1 0.0 copy-done
  89.1 0.7 copy.16
Async XLA Ops:
  86.1 1.8 %copy-start.1 = (f32[10,128]{1,0:T(8,128)S(1)}, f32[10,128]{1,0:T(8,128)}, u32[]{:S(2)}) copy-start(f32[10,128]{1,0:T(8,128)} %get-tuple-element.12) | copy-start | bytes 15364
  86.1 3.0 %copy-start = (f32[128,256]{1,0:T(8,128)S(1)}, f32[128,256]{1,0:T(8,128)}, u32[]{:S(2)}) copy-start(f32[128,256]{1,0:T(8,128)} %get-tuple-element.15) | copy-start | bytes 393220
  87.9 0.7 copy-start.2

commit v4 on v3

--- a/solution.py
+++ b/solution.py
@@ -67,10 +67,10 @@
     psi, pst, gt_acc, col_acc, weight,
     cs_send, cs_recv, rs_mid, rs_recv, gx_send, gx_recv, ga_send, ga_recv,
     gr_own, gr_all, yi_send, yi_recv, yt_send, yt_recv,
-    xi_send, xi_recv, xt_send, xt_recv, zi_sum, zt_sum, zi_send, zi_recv, zt_send, zt_recv,
+    term_i, term_t, zi_send, zi_recv, zt_send, zt_recv,
     in_ss, sq_ss, sq_rs, pp_ss, pp_rs, ig_ss, fw_ss, ig_rs, za_ss, za_rs,
     tx_ss, tx_rs, cs_ss, cs_rs, ri_ss, ri_rs, gx_ss, gx_rs, ga_ss, ga_rs,
-    gr_ss, gr_rs, yi_ss, yi_rs, yt_ss, yt_rs, x_ss, x_rs, zi_ss, zi_rs, zt_ss, zt_rs,
+    gr_ss, gr_rs, yi_ss, yi_rs, yt_ss, yt_rs, zi_ss, zi_rs, zt_ss, zt_rs,
 ):
     n_blocks = ny * XL
     n_plane = n_blocks * T
@@ -100,9 +100,6 @@
     def z_dev(other):
         return zt_dev(other, t)
 
-    def y_dev(other):
-        return ((other * Z + z) * XL + xl, t)
-
     def t_dev(other):
         return (dp, other)
 
@@ -157,6 +154,39 @@
 
     for i in range(1, T):
         sq_copy(i).start()
+
+    di4, dt4 = di // T, dt // T
+
+    def pp_pair(i, src, first):
+        other = (t + i) % T
+        quarter = pl.ds(pl.multiple_of(src * Q, Q), Q)
+        return (
+            remote(
+                imgp.at[pl.ds(pl.multiple_of(first * di4, 16), di4), :], psi.at[:, quarter],
+                pp_ss.at[2 * i], pp_rs.at[2 * src], t_dev(other),
+            ),
+            remote(
+                txtp.at[pl.ds(pl.multiple_of(first * dt4, 16), dt4), :], pst.at[:, quarter],
+                pp_ss.at[2 * i + 1], pp_rs.at[2 * src + 1], t_dev(other),
+            ),
+        )
+
+    def pp_copies(i):
+        return pp_pair(i, t, (t + i) % T)
+
+    for i in range(1, T):
+        for copy in pp_copies(i):
+            copy.start()
+    own_pp = [
+        pltpu.make_async_copy(
+            ref.at[pl.ds(pl.multiple_of(t * size, 16), size), :],
+            dst.at[:, pl.ds(pl.multiple_of(t * Q, Q), Q)], pp_ss.at[k],
+        )
+        for k, (ref, dst, size) in enumerate([(imgp, psi, di4), (txtp, pst, dt4)])
+    ]
+    for copy in own_pp:
+        copy.start()
+
     for i in range(1, T):
         src = (t + i) % T
         remote(sqb.at[src], sqb.at[src], sq_ss.at[i - 1], sq_rs.at[src], t_dev(src)).wait_recv()
@@ -211,9 +241,11 @@
             tx_local(k).start()
 
     far_first = sorted(range(1, na), key=lambda o: -min(o, na - o))
-    for o in far_first:
+    near_first = far_first[::-1]
+    near_groups = [o for o in near_first if min(o, na - o) == 1]
+    far_groups = [o for o in near_first if min(o, na - o) > 1]
+    for o in far_groups:
         za_copy(o).start()
-    pass_on(a)
 
     emb_img = (raw_img * as_columns(inv[0:1])).astype(bf16)
     own[0] = emb_img
@@ -246,9 +278,9 @@
         ig_copy(i).start()
 
     fw_own.start()
-    near_first = far_first[::-1]
-    near_groups = [o for o in near_first if min(o, na - o) == 1]
-    far_groups = [o for o in near_first if min(o, na - o) > 1]
+    for o in near_groups:
+        za_copy(o).start()
+    pass_on(a)
 
     mine = (t - c + T) % T
 
@@ -326,7 +358,9 @@
         za_land(o).wait_recv()
         pass_on((a + o) % na)
 
-    @pl.loop(1, n_half)
+    middle = n_half * 5 // 8
+
+    @pl.loop(1, middle)
     def _(i):
         ig_land(i).wait_recv()
         fw_copy(i).start()
@@ -334,6 +368,12 @@
     for o in far_groups:
         za_land(o).wait_recv()
         pass_on((a + o) % na)
+
+    @pl.loop(middle, n_half)
+    def _(i):
+        ig_land(i).wait_recv()
+        fw_copy(i).start()
+
     own_img_copy.wait()
 
     @pl.loop(0, n_half)
@@ -421,13 +461,13 @@
             sum(unpack(gx_recv[k * T + m, ROWS:PIECE, :]) for m in range(T))
         )
 
+    @pl.loop(0, n_blocks)
+    def _(n):
+        both_cores((b + 1 + n) % n_blocks)
+
     for o in near_groups:
         near_sum(o)
         ga_copy(o).start()
-
-    @pl.loop(0, n_blocks)
-    def _(n):
-        both_cores((b + 1 + n) % n_blocks)
 
     for o in far_groups:
         near_sum(o)
@@ -458,62 +498,60 @@
     diy, dty = di // ny, dt // ny
     per_i, per_t = diy // (Z * XL), dty // (Z * XL)
     win = window_of(per_i)
-
-    class Proj:
-        def __init__(self, feat, per_y, send, recv, ss, rs, x_send, x_recv, x_sem, zsum, m):
-            self.__dict__.update(locals())
-
-        def y_copy(self, i):
-            dst = (y + i) % ny
-            return remote(
-                self.send.at[pl.ds(pl.multiple_of(dst * self.per_y, 16), self.per_y)],
-                self.recv.at[y], self.ss.at[i], self.rs.at[y], y_dev(dst),
-            )
-
-        def x_copy(self):
-            return remote(
-                self.x_send, self.x_recv, x_ss.at[self.x_sem], x_rs.at[self.x_sem],
-                (dp - xl + (XL - 1 - xl), t),
-            )
-
-        def begin(self, grad):
-            gr_own[self.m] = grad
-            for k in range(0, self.feat.shape[1], 128):
-                self.send[k:k + 128, :] = tn(self.feat[:, k:k + 128], grad).astype(bf16)
-            for i in range(1, ny):
-                self.y_copy(i).start()
-
-        def middle(self):
-            self.zsum[...] = self.send[
-                pl.ds(pl.multiple_of(y * self.per_y, 16), self.per_y), :
-            ].astype(f32)
-            for i in range(1, ny):
-                src = (y + i) % ny
-                remote(
-                    self.send.at[pl.ds(0, self.per_y)], self.recv.at[src], self.ss.at[i],
-                    self.rs.at[src], y_dev(src),
-                ).wait_recv()
-            total = self.zsum[...]
-            for i in range(1, ny):
-                total += self.recv[(y + i) % ny].astype(f32)
-            self.zsum[...] = total
-            if XL == 2:
-                self.x_send[...] = total.astype(bf16)
-                self.x_copy().start()
-
-        def last(self):
-            if XL == 2:
-                self.x_copy().wait_recv()
-                self.zsum[...] += self.x_recv[...].astype(f32)
-
-        def finish(self):
-            for i in range(1, ny):
-                self.y_copy(i).wait_send()
-            if XL == 2:
-                self.x_copy().wait_send()
-
-    img = Proj(imgf, diy, yi_send, yi_recv, yi_ss, yi_rs, xi_send, xi_recv, 0, zi_sum, 0)
-    txt = Proj(txtf, dty, yt_send, yt_recv, yt_ss, yt_rs, xt_send, xt_recv, 1, zt_sum, 1)
+    pair = 2 if per_t % 16 else 1
+
+    def img_rows(block, other):
+        return (block // XL) * diy + ((other * XL + block % XL) * per_i) // 8 * 8
+
+    def txt_rows(block, other):
+        return (block // XL) * dty + (other * XL + block % XL) * per_t
+
+    def yi_copy(i):
+        dst = (b + i) % n_blocks
+        return remote(
+            yi_send.at[dst], yi_recv.at[b], yi_ss.at[i], yi_rs.at[b], plane_dev(dst * T + t)
+        )
+
+    def yt_copy(i):
+        dst = (b + i) % n_blocks
+        return remote(
+            yt_send.at[dst], yt_recv.at[b], yt_ss.at[i], yt_rs.at[b], plane_dev(dst * T + t)
+        )
+
+    def terms(feat, grad, term):
+        for k in range(0, feat.shape[1], 128):
+            term[k:k + 128, :] = tn(feat[:, k:k + 128], grad)
+
+    def img_begin(grad):
+        gr_own[0] = grad
+        terms(imgf, grad, term_i)
+        for block in range(n_blocks):
+            for other in range(Z):
+                first = img_rows(block, other)
+                yi_send[block, other] = term_i[first:first + win, :].astype(bf16)
+        for i in range(1, n_blocks):
+            yi_copy(i).start()
+
+    def txt_begin(grad):
+        gr_own[1] = grad
+        terms(txtf, grad, term_t)
+        for block in range(n_blocks):
+            for group in range(Z // pair):
+                rows = [
+                    term_t[txt_rows(block, group * pair + n):txt_rows(block, group * pair + n) + per_t, :]
+                    for n in range(pair)
+                ]
+                yt_send[block, group] = jnp.concatenate(rows, axis=0).astype(bf16)
+        for i in range(1, n_blocks):
+            yt_copy(i).start()
+
+    def plane_sum(send, recv, ss, rs):
+        total = send[b].astype(f32)
+        for i in range(1, n_blocks):
+            src = (b + i) % n_blocks
+            remote(send.at[0], recv.at[src], ss.at[i], rs.at[src], sibling).wait_recv()
+            total += recv[src].astype(f32)
+        return total
 
     def rs_sum(i, carry):
         total, sums = carry
@@ -531,7 +569,7 @@
     )
     own_img = own[0].astype(f32)
     own_txt = own[1].astype(f32)
-    img.begin(raw_grad(total_img, sums_img, own_img, own_txt, invr[0:1, :]))
+    img_begin(raw_grad(total_img, sums_img, own_img, own_txt, invr[0:1, :]))
 
     total_txt = ga_send[0, 0:ROWS, :].astype(f32)
     sums_txt = unpack(ga_send[0, ROWS:PIECE, :])
@@ -540,84 +578,44 @@
         remote(ga_send.at[0], ga_recv.at[src], ga_ss.at[o], ga_rs.at[src], sibling).wait_recv()
         total_txt += ga_recv[src, 0:ROWS, :].astype(f32)
         sums_txt += unpack(ga_recv[src, ROWS:PIECE, :])
-    txt.begin(raw_grad(total_txt, sums_txt, own_txt, own_img, invr[1:2, :]))
-
-    img.middle()
-    txt.middle()
+    txt_begin(raw_grad(total_txt, sums_txt, own_txt, own_img, invr[1:2, :]))
+
+    def zi_copy(i):
+        dst = (z + i) % Z
+        return remote(zi_send.at[dst], zi_recv.at[z], zi_ss.at[i], zi_rs.at[z], z_dev(dst))
+
+    def zt_copy(i):
+        dst = (z + i) % Z
+        return remote(zt_send.at[dst], zt_recv.at[z], zt_ss.at[i], zt_rs.at[z], z_dev(dst))
+
+    zi_send[...] = plane_sum(yi_send, yi_recv, yi_ss, yi_rs).astype(bf16)
+
+    @pl.loop(0, Z)
+    def _(n):
+        i = (Z // 2 + n) % Z
+
+        @pl.when(i > 0)
+        def _():
+            zi_copy(i).start()
+
+    total = plane_sum(yt_send, yt_recv, yt_ss, yt_rs)
+    for other in range(Z):
+        first = other % pair * per_t
+        rows = total[other // pair, first:first + per_t, :]
+        zt_send[other] = jnp.concatenate([rows] * pair, axis=0).astype(bf16)
+
+    @pl.loop(0, Z)
+    def _(n):
+        i = (Z // 2 + n) % Z
+
+        @pl.when(i > 0)
+        def _():
+            zt_copy(i).start()
 
     for m in range(2):
         own_gr[m].start()
         for i in range(1, T):
             gr_copy(m, i).start()
-    di4, dt4 = di // T, dt // T
-
-    def pp_pair(i, src, first):
-        other = (t + i) % T
-        quarter = pl.ds(pl.multiple_of(src * Q, Q), Q)
-        return (
-            remote(
-                imgp.at[pl.ds(pl.multiple_of(first * di4, 16), di4), :], psi.at[:, quarter],
-                pp_ss.at[2 * i], pp_rs.at[2 * src], t_dev(other),
-            ),
-            remote(
-                txtp.at[pl.ds(pl.multiple_of(first * dt4, 16), dt4), :], pst.at[:, quarter],
-                pp_ss.at[2 * i + 1], pp_rs.at[2 * src + 1], t_dev(other),
-            ),
-        )
-
-    def pp_copies(i):
-        return pp_pair(i, t, (t + i) % T)
-
-    for i in range(1, T):
-        for copy in pp_copies(i):
-            copy.start()
-    own_pp = [
-        pltpu.make_async_copy(
-            ref.at[pl.ds(pl.multiple_of(t * size, 16), size), :],
-            dst.at[:, pl.ds(pl.multiple_of(t * Q, Q), Q)], pp_ss.at[k],
-        )
-        for k, (ref, dst, size) in enumerate([(imgp, psi, di4), (txtp, pst, dt4)])
-    ]
-    for copy in own_pp:
-        copy.start()
-
-    def zi_copy(i):
-        dst = (z + i) % Z
-        return remote(zi_send.at[dst], zi_recv.at[z], zi_ss.at[i], zi_rs.at[z], z_dev(dst))
-
-    def zt_copy(i):
-        dst = (z + i) % Z
-        return remote(zt_send.at[dst], zt_recv.at[z], zt_ss.at[i], zt_rs.at[z], z_dev(dst))
-
-    img.last()
-
-    @pl.loop(0, Z)
-    def _(n):
-        i = (Z // 2 + n) % Z
-        dst = (z + i) % Z
-        first = ((dst * XL + xl) * per_i) // 8 * 8
-        zi_send[dst] = zi_sum[pl.ds(pl.multiple_of(first, 8), win), :].astype(bf16)
-
-        @pl.when(i > 0)
-        def _():
-            zi_copy(i).start()
-
-    txt.last()
-
-    @pl.loop(0, Z)
-    def _(n):
-        i = (Z // 2 + n) % Z
-        dst = (z + i) % Z
-        first = (dst * XL + xl) * per_t
-        block = zt_sum[pl.ds(pl.multiple_of(first, 8), per_t), :]
-        if per_t % 16:
-            block = jnp.concatenate([block, block], axis=0)
-        zt_send[dst] = block.astype(bf16)
-
-        @pl.when(i > 0)
-        def _():
-            zt_copy(i).start()
-
     for m in range(2):
         own_gr[m].wait()
         own_pp[m].wait()
@@ -687,8 +685,9 @@
             def _(quarter=quarter):
                 gx_copy(k, quarter).wait_send()
 
-    img.finish()
-    txt.finish()
+    for i in range(1, n_blocks):
+        yi_copy(i).wait_send()
+        yt_copy(i).wait_send()
 
     @pl.loop(1, Z)
     def _(i):
@@ -707,7 +706,9 @@
     ndp = ny * Z * XL
     diy, dty = di // ny, dt // ny
     win = window_of(diy // (Z * XL))
-    tall = max(dty // (Z * XL), 16)
+    per_t = dty // (Z * XL)
+    pair = 2 if per_t % 16 else 1
+    tall = per_t * pair
     dma = pltpu.SemaphoreType.DMA
     vmem = pltpu.VMEM
     piece = (PIECE, Q)
@@ -737,26 +738,22 @@
         vmem((na, *piece), bf16),
         vmem((2, ROWS, Q), bf16),
         vmem((2, ROWS, emb), bf16),
-        vmem((di, Q), bf16),
-        vmem((ny, diy, Q), bf16),
-        vmem((dt, Q), bf16),
-        vmem((ny, dty, Q), bf16),
-        vmem((diy, Q), bf16),
-        vmem((diy, Q), bf16),
-        vmem((dty, Q), bf16),
-        vmem((dty, Q), bf16),
-        vmem((diy, Q), f32),
-        vmem((dty, Q), f32),
+        vmem((n_blocks, Z, win, Q), bf16),
+        vmem((n_blocks, Z, win, Q), bf16),
+        vmem((n_blocks, Z // pair, pair * per_t, Q), bf16),
+        vmem((n_blocks, Z // pair, pair * per_t, Q), bf16),
+        vmem((di, Q), f32),
+        vmem((dt, Q), f32),
         vmem((Z, win, Q), bf16),
         vmem((Z, win, Q), bf16),
         vmem((Z, tall, Q), bf16),
         vmem((Z, tall, Q), bf16),
     ]
-    wide = max(ny, 2)
+    wide = max(n_blocks, 2)
     sems = [
         4, T, T, 2 * T, 2 * T, n_half, n_half, n_plane, na, na,
         na * T, na * T, n_blocks, n_blocks, n_half, n_half, na * T, na * T, na, na,
-        2 * T, 2 * T, wide, wide, wide, wide, 2, 2, Z, Z, Z, Z,
+        2 * T, 2 * T, wide, wide, wide, wide, Z, Z, Z, Z,
     ]
     scratch += [dma((n,)) for n in sems]
     whole = pl.BlockSpec(memory_space=pltpu.VMEM)

time: 90 us -> 88.6 us (0.984)
  Pallas kernels: 84.8 us -> 82.9 us
    pallas_call x1, Pallas kernels: 84.8 us -> 82.9 us  [shards(): pl.pallas_call(functools.partial(kernel, ny, di, dt), out_shape=(jax.Shap...]
where the time goes in v4:
time: 88.6 us; the launch traced here: 87.9 us
  Pallas kernels  82.9 us (94%)
  local copies, waits for them, and re-layouts  3.67 us (4%)
  between operations  1.31 us (1%)
    pallas_call x1, Pallas kernels, shards(): pl.pallas_call(functools.partial(kernel, ny, di, dt), out_shape=(jax.Shap...  82.9 us
    unnamed x9, local copies, waits for them, and re-layouts  1.93 us

profile of v4, /device:TPU:1, one launch (start us, length us, event | category | flops | bytes accessed | tf_op | source)
XLA Modules:
  0.0 87.9 jit_solution(1876426273997938364)
XLA Ops:
  1.3 82.9 %shard_map.84 = (f32[10,128]{1,0:T(8,128)}, f32[8,128]{1,0:T(8,128)}, f32[128,320]{1,0:T(8,128)}, f32[128,256]{1,0:T(8,128)}) custom-call(f32[1]{0:T(128)S(6)} %copy.13.scale_ref, bf16[128,1280]{1,0:T(8,128)(2,1)} %imgf_hbm.1, bf16[128,1024]{1,0:T(8,128)(2,1)} %txtf_hbm.1, bf16[1280,128]{1,0:T(8,128)(2,1)} %imgp_hbm.1, bf16[1024,128]{1,0:T(8,128)(2,1)} %txtp_hbm.1), custom_call_target="tpu_custom_call" | custom-call | tf_op jit(solution)/shard_map/pallas_call | solution.py:760
  84.2 0.0 copy-start.1
  84.2 0.0 copy-start
  84.2 1.7 %copy.9 = f32[128,320]{0,1:T(8,128)} copy(f32[128,320]{1,0:T(8,128)} %get-tuple-element.6) | data formatting | bytes 327680 | tf_op jit(solution)/shard_map/pallas_call | solution.py:760
  86.0 0.0 copy-done.1
  86.0 0.0 copy-start.2
  86.0 0.6 copy.14
  86.6 0.1 copy-done.2
  86.6 0.6 copy.15
  87.2 0.0 copy-done
  87.2 0.7 copy.16
Async XLA Ops:
  84.2 1.8 %copy-start.1 = (f32[10,128]{1,0:T(8,128)S(1)}, f32[10,128]{1,0:T(8,128)}, u32[]{:S(2)}) copy-start(f32[10,128]{1,0:T(8,128)} %get-tuple-element.12) | copy-start | bytes 15364
  84.2 3.0 %copy-start = (f32[128,256]{1,0:T(8,128)S(1)}, f32[128,256]{1,0:T(8,128)}, u32[]{:S(2)}) copy-start(f32[128,256]{1,0:T(8,128)} %get-tuple-element.15) | copy-start | bytes 393220
  86.0 0.7 copy-start.2

commit v5 on v4

--- a/solution.py
+++ b/solution.py
@@ -67,7 +67,7 @@
     psi, pst, gt_acc, col_acc, weight,
     cs_send, cs_recv, rs_mid, rs_recv, gx_send, gx_recv, ga_send, ga_recv,
     gr_own, gr_all, yi_send, yi_recv, yt_send, yt_recv,
-    term_i, term_t, zi_send, zi_recv, zt_send, zt_recv,
+    term_i, term_t, back_i, back_t, zi_send, zi_recv, zt_send, zt_recv,
     in_ss, sq_ss, sq_rs, pp_ss, pp_rs, ig_ss, fw_ss, ig_rs, za_ss, za_rs,
     tx_ss, tx_rs, cs_ss, cs_rs, ri_ss, ri_rs, gx_ss, gx_rs, ga_ss, ga_rs,
     gr_ss, gr_rs, yi_ss, yi_rs, yt_ss, yt_rs, zi_ss, zi_rs, zt_ss, zt_rs,
@@ -522,8 +522,14 @@
         for k in range(0, feat.shape[1], 128):
             term[k:k + 128, :] = tn(feat[:, k:k + 128], grad)
 
+    def share_grad(m):
+        own_gr[m].start()
+        for i in range(1, T):
+            gr_copy(m, i).start()
+
     def img_begin(grad):
         gr_own[0] = grad
+        share_grad(0)
         terms(imgf, grad, term_i)
         for block in range(n_blocks):
             for other in range(Z):
@@ -534,6 +540,7 @@
 
     def txt_begin(grad):
         gr_own[1] = grad
+        share_grad(1)
         terms(txtf, grad, term_t)
         for block in range(n_blocks):
             for group in range(Z // pair):
@@ -588,35 +595,7 @@
         dst = (z + i) % Z
         return remote(zt_send.at[dst], zt_recv.at[z], zt_ss.at[i], zt_rs.at[z], z_dev(dst))
 
-    zi_send[...] = plane_sum(yi_send, yi_recv, yi_ss, yi_rs).astype(bf16)
-
-    @pl.loop(0, Z)
-    def _(n):
-        i = (Z // 2 + n) % Z
-
-        @pl.when(i > 0)
-        def _():
-            zi_copy(i).start()
-
-    total = plane_sum(yt_send, yt_recv, yt_ss, yt_rs)
-    for other in range(Z):
-        first = other % pair * per_t
-        rows = total[other // pair, first:first + per_t, :]
-        zt_send[other] = jnp.concatenate([rows] * pair, axis=0).astype(bf16)
-
-    @pl.loop(0, Z)
-    def _(n):
-        i = (Z // 2 + n) % Z
-
-        @pl.when(i > 0)
-        def _():
-            zt_copy(i).start()
-
-    for m in range(2):
-        own_gr[m].start()
-        for i in range(1, T):
-            gr_copy(m, i).start()
-    for m in range(2):
+    def feature(m, back, rows, out):
         own_gr[m].wait()
         own_pp[m].wait()
         for i in range(1, T):
@@ -625,30 +604,24 @@
                 gr_own.at[m], gr_all.at[m, :, pl.ds(pl.multiple_of(src * Q, Q), Q)],
                 gr_ss.at[m * T + i], gr_rs.at[m * T + src], t_dev(src),
             ).wait_recv()
-    for i in range(1, T):
-        for copy in pp_pair(i, (t + i) % T, 0):
-            copy.wait_recv()
-    gif[...] = nt(gr_all[0], psi[...])
-    gtf[...] = nt(gr_all[1], pst[...])
-
-    def zi_add(i, total):
-        src = (z + i) % Z
-        remote(zi_send.at[0], zi_recv.at[src], zi_ss.at[i], zi_rs.at[src], sibling).wait_recv()
-        return total + zi_recv[src].astype(f32)
-
-    total = lax.fori_loop(1, Z, zi_add, zi_send[z].astype(f32))
-    shift = ((z * XL + xl) * per_i) % 8
-    result = total[0:per_i]
-    for k in sorted({(k * per_i) % 8 for k in range(8)} - {0}):
-        result = jnp.where(shift == k, total[k:k + per_i], result)
-    gip[...] = result
-
-    def zt_add(i, total):
-        src = (z + i) % Z
-        remote(zt_send.at[0], zt_recv.at[src], zt_ss.at[i], zt_rs.at[src], sibling).wait_recv()
-        return total + zt_recv[src, 0:per_t, :].astype(f32)
-
-    gtp[...] = lax.fori_loop(1, Z, zt_add, zt_send[z, 0:per_t, :].astype(f32))
+            pp_pair(i, src, 0)[m].wait_recv()
+        back[...] = nt(gr_all[m], rows[...])
+        copy = pltpu.make_async_copy(back, out, in_ss.at[m])
+        copy.start()
+        return copy
+
+    feature_out = [feature(0, back_i, psi, gif)]
+    zi_send[...] = plane_sum(yi_send, yi_recv, yi_ss, yi_rs).astype(bf16)
+
+    @pl.loop(0, Z)
+    def _(n):
+        i = (Z // 2 + n) % Z
+
+        @pl.when(i > 0)
+        def _():
+            zi_copy(i).start()
+
+    feature_out.append(feature(1, back_t, pst, gtf))
 
     for i in range(1, T):
         sq_copy(i).wait_send()
@@ -685,14 +658,49 @@
             def _(quarter=quarter):
                 gx_copy(k, quarter).wait_send()
 
+    total = plane_sum(yt_send, yt_recv, yt_ss, yt_rs)
+    for other in range(Z):
+        first = other % pair * per_t
+        rows = total[other // pair, first:first + per_t, :]
+        zt_send[other] = jnp.concatenate([rows] * pair, axis=0).astype(bf16)
+
+    @pl.loop(0, Z)
+    def _(n):
+        i = (Z // 2 + n) % Z
+
+        @pl.when(i > 0)
+        def _():
+            zt_copy(i).start()
+
     for i in range(1, n_blocks):
         yi_copy(i).wait_send()
         yt_copy(i).wait_send()
+
+    def zi_add(i, total):
+        src = (z + i) % Z
+        remote(zi_send.at[0], zi_recv.at[src], zi_ss.at[i], zi_rs.at[src], sibling).wait_recv()
+        return total + zi_recv[src].astype(f32)
+
+    total = lax.fori_loop(1, Z, zi_add, zi_send[z].astype(f32))
+    shift = ((z * XL + xl) * per_i) % 8
+    result = total[0:per_i]
+    for k in sorted({(k * per_i) % 8 for k in range(8)} - {0}):
+        result = jnp.where(shift == k, total[k:k + per_i], result)
+    gip[...] = result
+
+    def zt_add(i, total):
+        src = (z + i) % Z
+        remote(zt_send.at[0], zt_recv.at[src], zt_ss.at[i], zt_rs.at[src], sibling).wait_recv()
+        return total + zt_recv[src, 0:per_t, :].astype(f32)
+
+    gtp[...] = lax.fori_loop(1, Z, zt_add, zt_send[z, 0:per_t, :].astype(f32))
 
     @pl.loop(1, Z)
     def _(i):
         zi_copy(i).wait_send()
         zt_copy(i).wait_send()
+    for copy in feature_out:
+        copy.wait()
 
 
 def shards(ny, img_feat, txt_feat, img_proj, txt_proj, logit_scale):
@@ -744,6 +752,8 @@
         vmem((n_blocks, Z // pair, pair * per_t, Q), bf16),
         vmem((di, Q), f32),
         vmem((dt, Q), f32),
+        vmem((ROWS, di // T), f32),
+        vmem((ROWS, dt // T), f32),
         vmem((Z, win, Q), bf16),
         vmem((Z, win, Q), bf16),
         vmem((Z, tall, Q), bf16),
@@ -767,7 +777,7 @@
         ),
         in_specs=[pl.BlockSpec(memory_space=pltpu.SMEM)]
         + [pl.BlockSpec(memory_space=pl.ANY)] * 4,
-        out_specs=(whole,) * 4,
+        out_specs=(whole, whole) + (pl.BlockSpec(memory_space=pl.ANY),) * 2,
         scratch_shapes=scratch,
         compiler_params=pltpu.CompilerParams(
             collective_id=0, has_side_effects=True, vmem_limit_bytes=56 * 1024 * 1024

time: 88.6 us -> 89.8 us (1.014)
  Pallas kernels: 82.9 us -> 83.9 us
    pallas_call x1, Pallas kernels: 82.9 us -> 83.9 us  [shards(): pl.pallas_call(functools.partial(kernel, ny, di, dt), out_shape=(jax.Shap...]
where the time goes in v5:
time: 89.8 us; the launch traced here: 88.8 us
  Pallas kernels  83.9 us (93%)
  local copies, waits for them, and re-layouts  3.67 us (4%)
  between operations  1.31 us (1%)
    pallas_call x1, Pallas kernels, shards(): pl.pallas_call(functools.partial(kernel, ny, di, dt), out_shape=(jax.Shap...  83.9 us
    unnamed x9, local copies, waits for them, and re-layouts  1.93 us

profile of v5, /device:TPU:1, one launch (start us, length us, event | category | flops | bytes accessed | tf_op | source)
XLA Modules:
  0.0 88.8 jit_solution(9340352106146982072)
XLA Ops:
  1.3 83.9 %shard_map.84 = (f32[10,128]{1,0:T(8,128)}, f32[8,128]{1,0:T(8,128)}, f32[128,320]{1,0:T(8,128)}, f32[128,256]{1,0:T(8,128)}) custom-call(f32[1]{0:T(128)S(6)} %copy.13.scale_ref, bf16[128,1280]{1,0:T(8,128)(2,1)} %imgf_hbm.1, bf16[128,1024]{1,0:T(8,128)(2,1)} %txtf_hbm.1, bf16[1280,128]{1,0:T(8,128)(2,1)} %imgp_hbm.1, bf16[1024,128]{1,0:T(8,128)(2,1)} %txtp_hbm.1), custom_call_target="tpu_custom_call" | custom-call | tf_op jit(solution)/shard_map/pallas_call | solution.py:770
  85.1 0.0 copy-start.1
  85.2 0.0 copy-start
  85.2 1.7 %copy.9 = f32[128,320]{0,1:T(8,128)} copy(f32[128,320]{1,0:T(8,128)} %get-tuple-element.6) | data formatting | bytes 327680 | tf_op jit(solution)/shard_map/pallas_call | solution.py:770
  86.9 0.0 copy-done.1
  86.9 0.0 copy-start.2
  86.9 0.6 copy.14
  87.5 0.1 copy-done.2
  87.6 0.6 copy.15
  88.2 0.0 copy-done
  88.2 0.7 copy.16
Async XLA Ops:
  85.1 1.8 %copy-start.1 = (f32[10,128]{1,0:T(8,128)S(1)}, f32[10,128]{1,0:T(8,128)}, u32[]{:S(2)}) copy-start(f32[10,128]{1,0:T(8,128)} %get-tuple-element.12) | copy-start | bytes 15364
  85.2 3.0 %copy-start = (f32[128,256]{1,0:T(8,128)S(1)}, f32[128,256]{1,0:T(8,128)}, u32[]{:S(2)}) copy-start(f32[128,256]{1,0:T(8,128)} %get-tuple-element.15) | copy-start | bytes 393220
  86.9 0.7 copy-start.2

commit v6 on v5

--- a/solution.py
+++ b/solution.py
@@ -540,7 +540,6 @@
 
     def txt_begin(grad):
         gr_own[1] = grad
-        share_grad(1)
         terms(txtf, grad, term_t)
         for block in range(n_blocks):
             for group in range(Z // pair):
@@ -551,6 +550,7 @@
                 yt_send[block, group] = jnp.concatenate(rows, axis=0).astype(bf16)
         for i in range(1, n_blocks):
             yt_copy(i).start()
+        share_grad(1)
 
     def plane_sum(send, recv, ss, rs):
         total = send[b].astype(f32)
@@ -610,7 +610,6 @@
         copy.start()
         return copy
 
-    feature_out = [feature(0, back_i, psi, gif)]
     zi_send[...] = plane_sum(yi_send, yi_recv, yi_ss, yi_rs).astype(bf16)
 
     @pl.loop(0, Z)
@@ -620,6 +619,21 @@
         @pl.when(i > 0)
         def _():
             zi_copy(i).start()
+
+    feature_out = [feature(0, back_i, psi, gif)]
+    total = plane_sum(yt_send, yt_recv, yt_ss, yt_rs)
+    for other in range(Z):
+        first = other % pair * per_t
+        rows = total[other // pair, first:first + per_t, :]
+        zt_send[other] = jnp.concatenate([rows] * pair, axis=0).astype(bf16)
+
+    @pl.loop(0, Z)
+    def _(n):
+        i = (Z // 2 + n) % Z
+
+        @pl.when(i > 0)
+        def _():
+            zt_copy(i).start()
 
     feature_out.append(feature(1, back_t, pst, gtf))
 
@@ -657,20 +671,6 @@
             @pl.when((mine != 0) | (t != quarter))
             def _(quarter=quarter):
                 gx_copy(k, quarter).wait_send()
-
-    total = plane_sum(yt_send, yt_recv, yt_ss, yt_rs)
-    for other in range(Z):
-        first = other % pair * per_t
-        rows = total[other // pair, first:first + per_t, :]
-        zt_send[other] = jnp.concatenate([rows] * pair, axis=0).astype(bf16)
-
-    @pl.loop(0, Z)
-    def _(n):
-        i = (Z // 2 + n) % Z
-
-        @pl.when(i > 0)
-        def _():
-            zt_copy(i).start()
 
     for i in range(1, n_blocks):
         yi_copy(i).wait_send()

time: 89.8 us -> 88.7 us (0.988)
  Pallas kernels: 83.9 us -> 82.2 us
    pallas_call x1, Pallas kernels: 83.9 us -> 82.2 us  [shards(): pl.pallas_call(functools.partial(kernel, ny, di, dt), out_shape=(jax.Shap...]
where the time goes in v6:
time: 88.7 us; the launch traced here: 87.2 us
  Pallas kernels  82.2 us (93%)
  local copies, waits for them, and re-layouts  3.67 us (4%)
  between operations  1.31 us (1%)
    pallas_call x1, Pallas kernels, shards(): pl.pallas_call(functools.partial(kernel, ny, di, dt), out_shape=(jax.Shap...  82.2 us
    unnamed x9, local copies, waits for them, and re-layouts  1.93 us

profile of v6, /device:TPU:1, one launch (start us, length us, event | category | flops | bytes accessed | tf_op | source)
XLA Modules:
  0.0 87.2 jit_solution(15990407284282387900)
XLA Ops:
  1.3 82.2 %shard_map.84 = (f32[10,128]{1,0:T(8,128)}, f32[8,128]{1,0:T(8,128)}, f32[128,320]{1,0:T(8,128)}, f32[128,256]{1,0:T(8,128)}) custom-call(f32[1]{0:T(128)S(6)} %copy.13.scale_ref, bf16[128,1280]{1,0:T(8,128)(2,1)} %imgf_hbm.1, bf16[128,1024]{1,0:T(8,128)(2,1)} %txtf_hbm.1, bf16[1280,128]{1,0:T(8,128)(2,1)} %imgp_hbm.1, bf16[1024,128]{1,0:T(8,128)(2,1)} %txtp_hbm.1), custom_call_target="tpu_custom_call" | custom-call | tf_op jit(solution)/shard_map/pallas_call | solution.py:770
  83.5 0.0 copy-start.1
  83.5 0.0 copy-start
  83.5 1.7 %copy.9 = f32[128,320]{0,1:T(8,128)} copy(f32[128,320]{1,0:T(8,128)} %get-tuple-element.6) | data formatting | bytes 327680 | tf_op jit(solution)/shard_map/pallas_call | solution.py:770
  85.2 0.0 copy-done.1
  85.2 0.0 copy-start.2
  85.2 0.6 copy.14
  85.8 0.1 copy-done.2
  85.9 0.6 copy.15
  86.5 0.0 copy-done
  86.5 0.7 copy.16
Async XLA Ops:
  83.5 1.8 %copy-start.1 = (f32[10,128]{1,0:T(8,128)S(1)}, f32[10,128]{1,0:T(8,128)}, u32[]{:S(2)}) copy-start(f32[10,128]{1,0:T(8,128)} %get-tuple-element.12) | copy-start | bytes 15364
  83.5 3.0 %copy-start = (f32[128,256]{1,0:T(8,128)S(1)}, f32[128,256]{1,0:T(8,128)}, u32[]{:S(2)}) copy-start(f32[128,256]{1,0:T(8,128)} %get-tuple-element.15) | copy-start | bytes 393220
  85.2 0.7 copy-start.2

commit v7 on v6

--- a/solution.py
+++ b/solution.py
@@ -522,14 +522,8 @@
         for k in range(0, feat.shape[1], 128):
             term[k:k + 128, :] = tn(feat[:, k:k + 128], grad)
 
-    def share_grad(m):
-        own_gr[m].start()
-        for i in range(1, T):
-            gr_copy(m, i).start()
-
     def img_begin(grad):
         gr_own[0] = grad
-        share_grad(0)
         terms(imgf, grad, term_i)
         for block in range(n_blocks):
             for other in range(Z):
@@ -550,7 +544,6 @@
                 yt_send[block, group] = jnp.concatenate(rows, axis=0).astype(bf16)
         for i in range(1, n_blocks):
             yt_copy(i).start()
-        share_grad(1)
 
     def plane_sum(send, recv, ss, rs):
         total = send[b].astype(f32)
@@ -595,7 +588,35 @@
         dst = (z + i) % Z
         return remote(zt_send.at[dst], zt_recv.at[z], zt_ss.at[i], zt_rs.at[z], z_dev(dst))
 
-    def feature(m, back, rows, out):
+    zi_send[...] = plane_sum(yi_send, yi_recv, yi_ss, yi_rs).astype(bf16)
+
+    @pl.loop(0, Z)
+    def _(n):
+        i = (Z // 2 + n) % Z
+
+        @pl.when(i > 0)
+        def _():
+            zi_copy(i).start()
+
+    total = plane_sum(yt_send, yt_recv, yt_ss, yt_rs)
+    for other in range(Z):
+        first = other % pair * per_t
+        rows = total[other // pair, first:first + per_t, :]
+        zt_send[other] = jnp.concatenate([rows] * pair, axis=0).astype(bf16)
+
+    @pl.loop(0, Z)
+    def _(n):
+        i = (Z // 2 + n) % Z
+
+        @pl.when(i > 0)
+        def _():
+            zt_copy(i).start()
+
+    for m in range(2):
+        own_gr[m].start()
+        for i in range(1, T):
+            gr_copy(m, i).start()
+    for m in range(2):
         own_gr[m].wait()
         own_pp[m].wait()
         for i in range(1, T):
@@ -604,38 +625,17 @@
                 gr_own.at[m], gr_all.at[m, :, pl.ds(pl.multiple_of(src * Q, Q), Q)],
                 gr_ss.at[m * T + i], gr_rs.at[m * T + src], t_dev(src),
             ).wait_recv()
-            pp_pair(i, src, 0)[m].wait_recv()
-        back[...] = nt(gr_all[m], rows[...])
-        copy = pltpu.make_async_copy(back, out, in_ss.at[m])
+    for i in range(1, T):
+        for copy in pp_pair(i, (t + i) % T, 0):
+            copy.wait_recv()
+    back_i[...] = nt(gr_all[0], psi[...])
+    back_t[...] = nt(gr_all[1], pst[...])
+    feature_out = [
+        pltpu.make_async_copy(src, dst, in_ss.at[k])
+        for k, (src, dst) in enumerate([(back_i, gif), (back_t, gtf)])
+    ]
+    for copy in feature_out:
         copy.start()
-        return copy
-
-    zi_send[...] = plane_sum(yi_send, yi_recv, yi_ss, yi_rs).astype(bf16)
-
-    @pl.loop(0, Z)
-    def _(n):
-        i = (Z // 2 + n) % Z
-
-        @pl.when(i > 0)
-        def _():
-            zi_copy(i).start()
-
-    feature_out = [feature(0, back_i, psi, gif)]
-    total = plane_sum(yt_send, yt_recv, yt_ss, yt_rs)
-    for other in range(Z):
-        first = other % pair * per_t
-        rows = total[other // pair, first:first + per_t, :]
-        zt_send[other] = jnp.concatenate([rows] * pair, axis=0).astype(bf16)
-
-    @pl.loop(0, Z)
-    def _(n):
-        i = (Z // 2 + n) % Z
-
-        @pl.when(i > 0)
-        def _():
-            zt_copy(i).start()
-
-    feature_out.append(feature(1, back_t, pst, gtf))
 
     for i in range(1, T):
         sq_copy(i).wait_send()

time: 88.7 us -> 88.1 us (level); the launches traced: 87.2 us -> 87.7 us
  no operation moved by 1% of the time
where the time goes in v7:
time: 88.1 us; the launch traced here: 87.7 us
  Pallas kernels  82.8 us (94%)
  local copies, waits for them, and re-layouts  3.67 us (4%)
  between operations  1.31 us (1%)
    pallas_call x1, Pallas kernels, shards(): pl.pallas_call(functools.partial(kernel, ny, di, dt), out_shape=(jax.Shap...  82.8 us
    unnamed x9, local copies, waits for them, and re-layouts  1.93 us

profile of v7, /device:TPU:1, one launch (start us, length us, event | category | flops | bytes accessed | tf_op | source)
XLA Modules:
  0.0 87.7 jit_solution(13189480954498987390)
XLA Ops:
  1.3 82.8 %shard_map.84 = (f32[10,128]{1,0:T(8,128)}, f32[8,128]{1,0:T(8,128)}, f32[128,320]{1,0:T(8,128)}, f32[128,256]{1,0:T(8,128)}) custom-call(f32[1]{0:T(128)S(6)} %copy.13.scale_ref, bf16[128,1280]{1,0:T(8,128)(2,1)} %imgf_hbm.1, bf16[128,1024]{1,0:T(8,128)(2,1)} %txtf_hbm.1, bf16[1280,128]{1,0:T(8,128)(2,1)} %imgp_hbm.1, bf16[1024,128]{1,0:T(8,128)(2,1)} %txtp_hbm.1), custom_call_target="tpu_custom_call" | custom-call | tf_op jit(solution)/shard_map/pallas_call | solution.py:770
  84.0 0.0 copy-start.1
  84.0 0.0 copy-start
  84.1 1.7 %copy.9 = f32[128,320]{0,1:T(8,128)} copy(f32[128,320]{1,0:T(8,128)} %get-tuple-element.6) | data formatting | bytes 327680 | tf_op jit(solution)/shard_map/pallas_call | solution.py:770
  85.8 0.0 copy-done.1
  85.8 0.0 copy-start.2
  85.8 0.6 copy.14
  86.4 0.1 copy-done.2
  86.5 0.6 copy.15
  87.1 0.0 copy-done
  87.1 0.7 copy.16
Async XLA Ops:
  84.0 1.8 %copy-start.1 = (f32[10,128]{1,0:T(8,128)S(1)}, f32[10,128]{1,0:T(8,128)}, u32[]{:S(2)}) copy-start(f32[10,128]{1,0:T(8,128)} %get-tuple-element.12) | copy-start | bytes 15364
  84.0 3.0 %copy-start = (f32[128,256]{1,0:T(8,128)S(1)}, f32[128,256]{1,0:T(8,128)}, u32[]{:S(2)}) copy-start(f32[128,256]{1,0:T(8,128)} %get-tuple-element.15) | copy-start | bytes 393220
  85.8 0.7 copy-start.2

commit v8 on v7

--- a/solution.py
+++ b/solution.py
@@ -598,6 +598,11 @@
         def _():
             zi_copy(i).start()
 
+    for m in range(2):
+        own_gr[m].start()
+        for i in range(1, T):
+            gr_copy(m, i).start()
+
     total = plane_sum(yt_send, yt_recv, yt_ss, yt_rs)
     for other in range(Z):
         first = other % pair * per_t
@@ -612,10 +617,6 @@
         def _():
             zt_copy(i).start()
 
-    for m in range(2):
-        own_gr[m].start()
-        for i in range(1, T):
-            gr_copy(m, i).start()
     for m in range(2):
         own_gr[m].wait()
         own_pp[m].wait()

time: 88.1 us -> 89.4 us (1.015); the launches traced: 87.7 us -> 88 us
  no operation moved by 1% of the time
where the time goes in v8:
time: 89.4 us; the launch traced here: 88 us
  Pallas kernels  83 us (93%)
  local copies, waits for them, and re-layouts  3.67 us (4%)
  between operations  1.31 us (1%)
    pallas_call x1, Pallas kernels, shards(): pl.pallas_call(functools.partial(kernel, ny, di, dt), out_shape=(jax.Shap...  83 us
    unnamed x9, local copies, waits for them, and re-layouts  1.93 us

profile of v8, /device:TPU:1, one launch (start us, length us, event | category | flops | bytes accessed | tf_op | source)
XLA Modules:
  0.0 88.0 jit_solution(5287311060065268378)
XLA Ops:
  1.3 83.0 %shard_map.84 = (f32[10,128]{1,0:T(8,128)}, f32[8,128]{1,0:T(8,128)}, f32[128,320]{1,0:T(8,128)}, f32[128,256]{1,0:T(8,128)}) custom-call(f32[1]{0:T(128)S(6)} %copy.13.scale_ref, bf16[128,1280]{1,0:T(8,128)(2,1)} %imgf_hbm.1, bf16[128,1024]{1,0:T(8,128)(2,1)} %txtf_hbm.1, bf16[1280,128]{1,0:T(8,128)(2,1)} %imgp_hbm.1, bf16[1024,128]{1,0:T(8,128)(2,1)} %txtp_hbm.1), custom_call_target="tpu_custom_call" | custom-call | tf_op jit(solution)/shard_map/pallas_call | solution.py:771
  84.3 0.0 copy-start.1
  84.3 0.0 copy-start
  84.3 1.7 %copy.9 = f32[128,320]{0,1:T(8,128)} copy(f32[128,320]{1,0:T(8,128)} %get-tuple-element.6) | data formatting | bytes 327680 | tf_op jit(solution)/shard_map/pallas_call | solution.py:771
  86.1 0.0 copy-done.1
  86.1 0.0 copy-start.2
  86.1 0.6 copy.14
  86.7 0.1 copy-done.2
  86.8 0.6 copy.15
  87.3 0.0 copy-done
  87.3 0.7 copy.16
Async XLA Ops:
  84.3 1.8 %copy-start.1 = (f32[10,128]{1,0:T(8,128)S(1)}, f32[10,128]{1,0:T(8,128)}, u32[]{:S(2)}) copy-start(f32[10,128]{1,0:T(8,128)} %get-tuple-element.12) | copy-start | bytes 15364
  84.3 3.0 %copy-start = (f32[128,256]{1,0:T(8,128)S(1)}, f32[128,256]{1,0:T(8,128)}, u32[]{:S(2)}) copy-start(f32[128,256]{1,0:T(8,128)} %get-tuple-element.15) | copy-start | bytes 393220
  86.1 0.7 copy-start.2
